TPU v7x, 32 devices: a whole 2x2x4 slice. The times are simulated.
32 devices in a mesh: ctx: 4 (over x, core), exp: 8 (over z, y).
Axes of the slice: x: 2, y: 2, z: 4, core: 2. Of those that a mesh axis runs over, the one named last changes fastest.
Arguments:
- residual: bfloat16 [8, 512, 1024], P('exp', 'ctx'), may hold values from -6 to 6
- query_rows: bfloat16 [8, 512, 1024], P('exp', 'ctx'), may hold values from -8 to 8
- key_rows: bfloat16 [8, 512, 1024], P('exp', 'ctx'), may hold values from -4 to 4
- value_rows: bfloat16 [8, 512, 1024], P('exp', 'ctx'), may hold values from -6 to 6
- out_proj: bfloat16 [1024, 1024], P('exp'), may hold values from -0.75 to 0.75
- router: bfloat16 [1024, 8], replicated, may hold values from -0.5 to 0.5
- expert_ids: int32 [8, 512, 2], P('exp', 'ctx'), may hold values from 0 to 7, all different within a row; in each aligned block of 128 rows (0 to 127, 128 to 255, ..., all dimensions but the last counted through in order) at most 48 rows name the same one
- expert_gate_up: bfloat16 [8, 1024, 1536], P('exp', 'ctx'), may hold values from -0.1875 to 0.1875
- expert_down: bfloat16 [8, 768, 1024], P('exp', 'ctx'), may hold values from -0.21875 to 0.21875
Outputs:
- layer_out: bfloat16 [8, 512, 1024], P('exp', 'ctx')
Inputs may be any that keep to these rules, and one draw needn't show every extreme that they name: `expert_ids`: the 2 ids of a token differ. Among the 128 tokens of one device (aligned blocks of 128 tokens of the flattened sequences) each expert is named at most 48 times, a bound that some block reaches.
All inputs are finite; a program needn't handle non-finite values.
Results may differ from a plain program's by a relative error of at most 0.017.
Values may be sent and summed in bfloat16 or wider, within the bound.
A program may use at most 64 MiB of HBM per device.

v0:
```python
import jax
import jax.numpy as jnp
from jax import lax
from jax.sharding import PartitionSpec as P

HEADS = 8
HEAD_DIM = 128
TOP = 2


NEG_FILL = -1e30


def attend_moving_queries(work_queries, key_rows, value_rows, cycle_index, scale_factor):
    token_count = work_queries.shape[0]
    cycle_size = lax.axis_size("ctx")
    gathered = lax.all_gather(work_queries[None], "ctx", axis=1, tiled=True)[0]
    row_count = gathered.shape[0]
    row_ids = jnp.arange(row_count, dtype=jnp.int32)
    query_heads = gathered.reshape(row_count, HEADS, HEAD_DIM)
    key_heads = key_rows[0].reshape(token_count, HEADS, HEAD_DIM)
    value_heads = value_rows[0].reshape(token_count, HEADS, HEAD_DIM)
    key_pos = cycle_index * token_count + jnp.arange(token_count, dtype=jnp.int32)
    scores = (
        jnp.einsum("qhd,khd->qhk", query_heads, key_heads, preferred_element_type=jnp.float32)
        * scale_factor
    )
    allowed = key_pos[None, None, :] <= row_ids[:, None, None]
    part_max = jnp.max(jnp.where(allowed, scores, NEG_FILL), axis=2)
    weights = jnp.where(allowed, jnp.exp(scores - part_max[:, :, None]), 0.0)
    part_sum = jnp.sum(weights, axis=2)
    part_acc = jnp.einsum(
        "qhk,khd->qhd",
        weights.astype(jnp.bfloat16),
        value_heads,
        preferred_element_type=jnp.float32,
    )
    got_acc, got_max, got_sum = (
        lax.all_to_all(
            part_acc.astype(jnp.bfloat16), "ctx", split_axis=0, concat_axis=0, tiled=True
        ).astype(part_acc.dtype),
        lax.all_to_all(
            part_max.astype(jnp.bfloat16), "ctx", split_axis=0, concat_axis=0, tiled=True
        ).astype(part_max.dtype),
        lax.all_to_all(
            part_sum.astype(jnp.bfloat16), "ctx", split_axis=0, concat_axis=0, tiled=True
        ).astype(part_sum.dtype),
    )
    got_acc = got_acc.reshape(cycle_size, token_count, HEADS, HEAD_DIM)
    got_max = got_max.reshape(cycle_size, token_count, HEADS)
    got_sum = got_sum.reshape(cycle_size, token_count, HEADS)
    top_max = jnp.max(got_max, axis=0)
    factor = jnp.exp(got_max - top_max[None])
    run_sum = jnp.sum(factor * got_sum, axis=0)
    run_acc = jnp.sum(factor[:, :, :, None] * got_acc, axis=0)
    return (
        (run_acc / run_sum[:, :, None]).reshape(token_count, HEADS * HEAD_DIM).astype(jnp.bfloat16)
    )


def on_device(
    residual,
    query_rows,
    key_rows,
    value_rows,
    out_proj,
    router,
    expert_ids,
    expert_gate_up,
    expert_down,
):
    token_count = residual.shape[1]
    model_width = residual.shape[2]
    cycle_index = lax.axis_index("ctx")
    scale_factor = HEAD_DIM ** (-0.5)
    local_queries = query_rows[0]
    context_rows = attend_moving_queries(
        local_queries, key_rows, value_rows, cycle_index, scale_factor
    )
    attn_out = jnp.dot(
        context_rows,
        lax.all_gather(out_proj, "exp", axis=0, tiled=True),
        preferred_element_type=jnp.float32,
    )
    hidden_state = (residual[0].astype(jnp.float32) + attn_out).astype(jnp.bfloat16)
    hidden_wide = hidden_state.astype(jnp.float32)
    mean_square = jnp.mean(hidden_wide * hidden_wide, axis=1, keepdims=True)
    normed = (hidden_wide * lax.rsqrt(mean_square + 1e-06)).astype(jnp.bfloat16)
    affinity = jax.nn.sigmoid(jnp.dot(normed, router, preferred_element_type=jnp.float32))
    chosen_ids = expert_ids[0]
    picked = jnp.take_along_axis(affinity, chosen_ids, axis=1)
    gate_share = picked / jnp.sum(picked, axis=1, keepdims=True)
    expert_count = router.shape[1]
    capacity = min(token_count, 3 * token_count // lax.axis_size("exp"))
    pair_ids = chosen_ids.reshape(token_count * TOP)
    one_hot = (pair_ids[:, None] == jnp.arange(expert_count, dtype=jnp.int32)[None, :]).astype(
        jnp.int32
    )
    earlier = jnp.cumsum(one_hot, axis=0) - one_hot
    slot_index = jnp.sum(earlier * one_hot, axis=1)
    target = pair_ids * capacity + slot_index
    slot_grid = jnp.arange(expert_count * capacity, dtype=jnp.int32)
    dispatch = jnp.any(
        slot_grid[:, None, None] == target.reshape(token_count, TOP)[None], axis=2
    ).astype(jnp.bfloat16)
    outgoing = jnp.dot(dispatch, normed, preferred_element_type=jnp.float32).astype(jnp.bfloat16)
    outgoing = outgoing.reshape(expert_count, capacity, model_width)
    full_gate_up, full_down = (
        lax.all_gather(expert_gate_up, "ctx", axis=1, tiled=True),
        lax.all_gather(expert_down, "ctx", axis=1, tiled=True),
    )
    ff_width = full_down.shape[1]
    arrived = lax.all_to_all(outgoing, "exp", split_axis=0, concat_axis=0, tiled=True)
    flat_feats = arrived.reshape(-1, model_width)
    gate_up_out = jnp.dot(flat_feats, full_gate_up[0], preferred_element_type=jnp.float32)
    activation = (jax.nn.silu(gate_up_out[:, :ff_width]) * gate_up_out[:, ff_width:]).astype(
        jnp.bfloat16
    )
    produced = jnp.dot(activation, full_down[0], preferred_element_type=jnp.float32).astype(
        jnp.bfloat16
    )
    returned_rows = lax.all_to_all(
        produced.reshape(arrived.shape), "exp", split_axis=0, concat_axis=0, tiled=True
    )
    flat_back = returned_rows.reshape(expert_count * capacity, model_width)
    pair_out = (
        jnp.take(flat_back, target, axis=0)
        .reshape(token_count, TOP, model_width)
        .astype(jnp.float32)
    )
    moe_out = jnp.sum(gate_share[:, :, None] * pair_out, axis=1)
    return (hidden_wide + moe_out).astype(jnp.bfloat16)[None]


def solution(mesh):
    return jax.shard_map(
        on_device,
        mesh=mesh,
        in_specs=(
            P("exp", "ctx", None),
            P("exp", "ctx", None),
            P("exp", "ctx", None),
            P("exp", "ctx", None),
            P("exp", None),
            P(),
            P("exp", "ctx", None),
            P("exp", "ctx", None),
            P("exp", "ctx", None),
        ),
        out_specs=P("exp", "ctx", None),
        check_vma=False,
    )
```

profile of v0, /device:TPU:0, one launch (start us, length us, event | category | flops | bytes accessed | tf_op | source)
XLA Modules:
  0.0 169.9 jit_solution(3516479571944432388)
XLA Ops:
  6.6 1.8 %copy.55 = bf16[1,128,1024]{1,2,0:T(8,128)(2,1)} copy(bf16[1,128,1024]{2,1,0:T(8,128)(2,1)} %param.10) | data formatting | bytes 524288 | tf_op args[1]
  8.5 0.7 all-gather.7.cloned.1.call-update
  9.3 0.7 all-gather.9.cloned.1.call-update
  10.0 0.5 all-gather.11.cloned.1.call-update
  10.5 0.1 copy.64
  10.6 0.1 eq.41
  10.8 0.1 reshape_squeeze.15
  11.2 0.6 reduce-window.6
  11.8 16.7 %all-gather.5.cloned.1.call-done = bf16[1,512,1024]{1,2,0:T(8,128)(2,1)} async-done(((bf16[1,128,1024]{1,2,0:T(8,128)(2,1)}), bf16[1,512,1024]{1,2,0:T(8,128)(2,1)}) %all-gather.5.cloned.1.call-update) | async-done | bytes 1048592 | tf_op jit(solution)/shard_map/all_gather | solution.py:17
  28.5 1.8 %fusion.2 = (f32[512,8]{0,1:T(8,128)S(1)}, f32[8,128,512]{2,1,0:T(8,128)S(1)}) fusion(pred[512,128]{0,1:T(8,128)(4,1)S(1)} %iota_compare_fusion.1, bf16[512,8,128]{0,2,1:T(8,128)(2,1)} %bitcast.87, bf16[128,8,128]{2,1,0:T(8,128)(2,1)S(1)} %bitcast.88), kind=kOutput, calls=%fused_computation.6 | convolution fusion | flops 135786496 | bytes 3489792 | tf_op jit(solution)/shard_map/qhd,khd->qhk/dot_general | solution.py:25
  30.3 1.1 fusion.6
  31.3 3.2 %all-to-all-start.2 = ((bf16[4,128,8]{1,2,0:T(8,128)(2,1)}), bf16[4,128,8]{1,2,0:T(8,128)(2,1)S(1)}, u32[]{:S(2)}, u32[]{:S(2)}) async-start(bf16[4,128,8]{1,2,0:T(8,128)(2,1)} %bitcast.79), calls=%async_computation.2 | async-start | bytes 16384 | tf_op jit(solution)/shard_map/all_to_all | solution.py:45
  34.6 0.6 convert_bitcast_fusion.1
  35.2 3.2 %all-to-all-done.2 = bf16[4,128,8]{1,2,0:T(8,128)(2,1)S(1)} async-done(((bf16[4,128,8]{1,2,0:T(8,128)(2,1)}), bf16[4,128,8]{1,2,0:T(8,128)(2,1)S(1)}, u32[]{:S(2)}, u32[]{:S(2)}) %all-to-all-start.2) | async-done | bytes 8224 | tf_op jit(solution)/shard_map/all_to_all | solution.py:45
  38.4 3.2 %all-to-all-start = ((bf16[4,128,8]{1,2,0:T(8,128)(2,1)}), bf16[4,128,8]{1,2,0:T(8,128)(2,1)S(1)}, u32[]{:S(2)}, u32[]{:S(2)}) async-start(bf16[4,128,8]{1,2,0:T(8,128)(2,1)} %convert_bitcast_fusion.1), calls=%async_computation | async-start | bytes 16384 | tf_op jit(solution)/shard_map/all_to_all | solution.py:42
  41.6 0.8 fusion.13
  42.4 1.6 copy.61
  44.0 1.4 all-to-all-done
  45.4 3.5 %all-to-all-start.1 = ((bf16[512,8,128]{2,1,0:T(8,128)(2,1)}), bf16[512,8,128]{2,1,0:T(8,128)(2,1)S(1)}, u32[]{:S(2)}, u32[]{:S(2)}) async-start(bf16[512,8,128]{2,1,0:T(8,128)(2,1)} %copy.61), calls=%async_computation.1 | async-start | bytes 2097152 | tf_op jit(solution)/shard_map/all_to_all | solution.py:39
  48.9 0.2 slice_reduce_fusion
  49.3 0.1 reduce_sum.76
  49.6 13.7 %all-to-all-done.1 = bf16[512,8,128]{2,1,0:T(8,128)(2,1)S(1)} async-done(((bf16[512,8,128]{2,1,0:T(8,128)(2,1)}), bf16[512,8,128]{2,1,0:T(8,128)(2,1)S(1)}, u32[]{:S(2)}, u32[]{:S(2)}) %all-to-all-start.1) | async-done | bytes 1048608 | tf_op jit(solution)/shard_map/all_to_all | solution.py:39
  63.3 0.1 bitcast_convert_fusion
  63.5 0.8 fusion.5
  64.3 0.2 divide_convert_fusion
  64.5 0.2 copy.63
  64.7 15.3 %all-gather.7.cloned.1.call-done = bf16[1024,1024]{1,0:T(8,128)(2,1)} async-done(((bf16[128,1024]{1,0:T(8,128)(2,1)}), bf16[1024,1024]{1,0:T(8,128)(2,1)}) %all-gather.7.cloned.1.call-update) | async-done | bytes 2097168 | tf_op jit(solution)/shard_map/all_gather | solution.py:82
  80.0 2.1 %multiply_reduce_fusion.1 = (f32[128]{0:T(128)S(1)}, f32[128,1024]{1,0:T(8,128)S(1)}) fusion(bf16[128,1024]{0,1:T(8,128)(2,1)S(1)} %bitcast.89, bf16[1024,1024]{1,0:T(8,128)(2,1)} %all-gather.7.cloned.1.call-done, bf16[1,128,1024]{2,1,0:T(8,128)(2,1)S(1)} %copy-done.3), kind=kOutput, calls=%fused_computation.37 | convolution fusion | flops 269221760 | bytes 3146240 | tf_op jit(solution)/shard_map/dot_general | solution.py:80
  82.1 1.3 convolution_convert_fusion.1
  83.4 3.6 %all-to-all-start.3 = ((bf16[8,48,1024]{2,1,0:T(8,128)(2,1)}), bf16[8,48,1024]{2,1,0:T(8,128)(2,1)S(1)}, u32[]{:S(2)}, u32[]{:S(2)}) async-start(bf16[8,48,1024]{2,1,0:T(8,128)(2,1)} %bitcast.13), calls=%async_computation.3 | async-start | bytes 1572864 | tf_op jit(solution)/shard_map/all_to_all | solution.py:113
  87.0 21.6 %all-gather.9.cloned.1.call-done = bf16[1,1024,1536]{2,1,0:T(8,128)(2,1)} async-done(((bf16[1,256,1536]{2,1,0:T(8,128)(2,1)}), bf16[1,1024,1536]{2,1,0:T(8,128)(2,1)}) %all-gather.9.cloned.1.call-update) | async-done | bytes 3145744 | tf_op jit(solution)/shard_map/all_gather | solution.py:109
  108.6 4.7 %fusion = f32[384,1536]{1,0:T(8,128)} fusion(bf16[384,1024]{1,0:T(8,128)(2,1)S(1)} %bitcast.90, bf16[1,1024,1536]{2,1,0:T(8,128)(2,1)} %all-gather.9.cloned.1.call-done), kind=kOutput, calls=%fused_computation.2 | convolution fusion | flops 1207959552 | bytes 6291456 | tf_op jit(solution)/shard_map/dot_general | solution.py:115
  113.3 16.4 %all-gather.11.cloned.1.call-done = bf16[1,768,1024]{2,1,0:T(8,128)(2,1)} async-done(((bf16[1,192,1024]{2,1,0:T(8,128)(2,1)}), bf16[1,768,1024]{2,1,0:T(8,128)(2,1)}) %all-gather.11.cloned.1.call-update) | async-done | bytes 1572880 | tf_op jit(solution)/shard_map/all_gather | solution.py:110
  129.7 3.8 %fusion.10 = bf16[384,1024]{1,0:T(8,128)(2,1)} fusion(bf16[1,768,1024]{2,1,0:T(8,128)(2,1)} %all-gather.11.cloned.1.call-done, f32[384,1536]{1,0:T(8,128)} %fusion), kind=kOutput, calls=%fused_computation.16 | convolution fusion | flops 606142464 | bytes 4718592 | tf_op jit(solution)/shard_map/dot_general | solution.py:119
  133.5 5.5 %all-to-all-start.4 = ((bf16[8,48,1024]{2,1,0:T(8,128)(2,1)}), bf16[8,48,1024]{2,1,0:T(8,128)(2,1)S(1)}, u32[]{:S(2)}, u32[]{:S(2)}) async-start(bf16[8,48,1024]{2,1,0:T(8,128)(2,1)} %bitcast.17), calls=%async_computation.4 | async-start | bytes 1572864 | tf_op jit(solution)/shard_map/all_to_all | solution.py:122
  139.0 0.1 reduce_sum.75
  139.2 0.1 copy.65
  139.3 0.1 reshape.217
  139.4 0.1 mul.94
  139.7 0.2 fusion.19
  139.9 1.4 gather_fusion.1
  141.3 0.1 reshape.220
  141.4 0.1 fusion.36
  141.7 17.9 %all-to-all-done.4 = bf16[8,48,1024]{2,1,0:T(8,128)(2,1)S(1)} async-done(((bf16[8,48,1024]{2,1,0:T(8,128)(2,1)}), bf16[8,48,1024]{2,1,0:T(8,128)(2,1)S(1)}, u32[]{:S(2)}, u32[]{:S(2)}) %all-to-all-start.4) | async-done | bytes 786464 | tf_op jit(solution)/shard_map/all_to_all | solution.py:122
  159.6 1.2 gather_fusion
  160.7 0.2 gather.12
  160.9 1.6 multiply_reduce_fusion
  162.6 0.8 fusion.28
  (37 shorter events, 0.9 us)
Async XLA Ops:
  6.5 133.1 %copy-start = (bf16[1024,8]{0,1:T(8,128)(2,1)S(1)}, bf16[1024,8]{0,1:T(8,128)(2,1)}, u32[]{:S(2)}) copy-start(bf16[1024,8]{0,1:T(8,128)(2,1)} %param.14) | copy-start | bytes 49156
  6.5 4.0 %copy-start.4 = (s32[1,128,2]{1,2,0:T(2,128)S(1)}, s32[1,128,2]{1,2,0:T(2,128)}, u32[]{:S(2)}) copy-start(s32[1,128,2]{1,2,0:T(2,128)} %param.15) | copy-start | bytes 3076
  6.5 4.5 %copy-start.1 = (bf16[1,128,1024]{2,1,0:T(8,128)(2,1)S(1)}, bf16[1,128,1024]{2,1,0:T(8,128)(2,1)}, u32[]{:S(2)}) copy-start(bf16[1,128,1024]{2,1,0:T(8,128)(2,1)} %param.11) | copy-start | bytes 786436
  6.5 4.6 %copy-start.2 = (bf16[1,128,1024]{2,1,0:T(8,128)(2,1)S(1)}, bf16[1,128,1024]{2,1,0:T(8,128)(2,1)}, u32[]{:S(2)}) copy-start(bf16[1,128,1024]{2,1,0:T(8,128)(2,1)} %param.12) | copy-start | bytes 786436
  6.5 22.0 %all-gather.5.cloned.1.call-start = ((), (), s32[]{:S(2)}) async-start(), calls=%async_computation.5 | async-start | bytes 1310720 | tf_op jit(solution)/shard_map/all_gather | solution.py:17
  8.5 71.5 %all-gather.7.cloned.1.call-start = ((), (), s32[]{:S(2)}) async-start(), calls=%async_computation.6 | async-start | bytes 2359296 | tf_op jit(solution)/shard_map/all_gather | solution.py:82
  9.2 99.4 %all-gather.9.cloned.1.call-start = ((), (), s32[]{:S(2)}) async-start(), calls=%async_computation.7 | async-start | bytes 3932160 | tf_op jit(solution)/shard_map/all_gather | solution.py:109
  9.9 119.7 %all-gather.11.cloned.1.call-start = ((), (), s32[]{:S(2)}) async-start(), calls=%async_computation.8 | async-start | bytes 1966080 | tf_op jit(solution)/shard_map/all_gather | solution.py:110
  31.3 7.0 %all-to-all-start.2 = ((bf16[4,128,8]{1,2,0:T(8,128)(2,1)}), bf16[4,128,8]{1,2,0:T(8,128)(2,1)S(1)}, u32[]{:S(2)}, u32[]{:S(2)}) async-start(bf16[4,128,8]{1,2,0:T(8,128)(2,1)} %bitcast.79), calls=%async_computation.2 | async-start | bytes 16384 | tf_op jit(solution)/shard_map/all_to_all | solution.py:45
  38.4 7.0 %all-to-all-start = ((bf16[4,128,8]{1,2,0:T(8,128)(2,1)}), bf16[4,128,8]{1,2,0:T(8,128)(2,1)S(1)}, u32[]{:S(2)}, u32[]{:S(2)}) async-start(bf16[4,128,8]{1,2,0:T(8,128)(2,1)} %convert_bitcast_fusion.1), calls=%async_computation | async-start | bytes 16384 | tf_op jit(solution)/shard_map/all_to_all | solution.py:42
  45.4 18.0 %all-to-all-start.1 = ((bf16[512,8,128]{2,1,0:T(8,128)(2,1)}), bf16[512,8,128]{2,1,0:T(8,128)(2,1)S(1)}, u32[]{:S(2)}, u32[]{:S(2)}) async-start(bf16[512,8,128]{2,1,0:T(8,128)(2,1)} %copy.61), calls=%async_computation.1 | async-start | bytes 2097152 | tf_op jit(solution)/shard_map/all_to_all | solution.py:39
  63.5 16.5 %copy-start.3 = (bf16[1,128,1024]{2,1,0:T(8,128)(2,1)S(1)}, bf16[1,128,1024]{2,1,0:T(8,128)(2,1)}, u32[]{:S(2)}) copy-start(bf16[1,128,1024]{2,1,0:T(8,128)(2,1)} %param.9) | copy-start | bytes 786436
  83.4 25.1 %all-to-all-start.3 = ((bf16[8,48,1024]{2,1,0:T(8,128)(2,1)}), bf16[8,48,1024]{2,1,0:T(8,128)(2,1)S(1)}, u32[]{:S(2)}, u32[]{:S(2)}) async-start(bf16[8,48,1024]{2,1,0:T(8,128)(2,1)} %bitcast.13), calls=%async_computation.3 | async-start | bytes 1572864 | tf_op jit(solution)/shard_map/all_to_all | solution.py:113
  133.5 26.1 %all-to-all-start.4 = ((bf16[8,48,1024]{2,1,0:T(8,128)(2,1)}), bf16[8,48,1024]{2,1,0:T(8,128)(2,1)S(1)}, u32[]{:S(2)}, u32[]{:S(2)}) async-start(bf16[8,48,1024]{2,1,0:T(8,128)(2,1)} %bitcast.17), calls=%async_computation.4 | async-start | bytes 1572864 | tf_op jit(solution)/shard_map/all_to_all | solution.py:122
Sparse Core Ops, SparseCore 0:
  8.9 19.5 all-gather.4
  30.6 49.2 all-gather.6
  81.5 27.0 all-gather.8
  110.0 19.6 all-gather.10
where the time goes:
time: 170 us
  waiting for transfers between devices  108 us (64%)
  starting transfers between devices  19.2 us (11%)
  matrix products  14.8 us (9%)
  between operations  13.4 us (8%)
  local copies, waits for them, and re-layouts  8.02 us (5%)
  other arithmetic  6.39 us (4%)
    all_gather x1, waiting for transfers between devices, on_device(): lax.all_gather(expert_gate_up, 'ctx', axis=1, tiled=True)  21.6 us
    all_to_all x1, waiting for transfers between devices, on_device(): lax.all_to_all(produced.reshape(arrived.shape), 'exp', split_axis=0, conc...  17.9 us
    all_gather x1, waiting for transfers between devices, attend_moving_queries(): gathered = lax.all_gather(work_queries[None], 'ctx', axis=1, tiled=True)[0]  16.7 us
    all_gather x1, waiting for transfers between devices, on_device(): lax.all_gather(expert_down, 'ctx', axis=1, tiled=True)  16.4 us
    all_gather x1, waiting for transfers between devices, on_device(): lax.all_gather(out_proj, 'exp', axis=0, tiled=True)  15.3 us
    all_to_all x1, waiting for transfers between devices, attend_moving_queries(): lax.all_to_all(part_acc.astype(jnp.bfloat16), 'ctx', split_axis=0, concat...  13.7 us
    all_to_all x1, starting transfers between devices, on_device(): lax.all_to_all(produced.reshape(arrived.shape), 'exp', split_axis=0, conc...  5.52 us
    dot_general x1, matrix products, on_device(): jnp.dot(flat_feats, full_gate_up[0], preferred_element_type=jnp.float32)  4.74 us
  transfers between devices with their start and end apart: 9, of which 8 were waited for; matrix products, arithmetic and copies ran while one was open for 12% of the time, Pallas kernels for 0%

commit v1 on v0

v1 whole, which is shorter than its diff:
```python
import functools

import jax
import jax.numpy as jnp
from jax import lax
from jax.experimental import pallas as pl
from jax.experimental.pallas import tpu as pltpu
from jax.sharding import PartitionSpec as P

HEADS = 8
HEAD_DIM = 128
NEG_FILL = -1e30
MESH = pl.DeviceIdType.MESH


def fused(
    n_ctx,
    n_exp,
    cap,
    residual,
    query,
    router,
    ids_ref,
    key,
    value,
    out_proj,
    gate_up,
    down,
    out,
    kbuf,
    vbuf,
    proj,
    gbuf,
    dbuf,
    outgoing,
    arrived,
    produced,
    returned,
    context,
    activation,
    local_sem,
    k_send,
    k_recv,
    v_send,
    v_recv,
    g_send,
    g_recv,
    d_send,
    d_recv,
    proj_send,
    proj_recv,
    proj_fwd,
    out_send,
    out_recv,
    back_send,
    back_recv,
):
    chips = n_ctx // 2
    c = lax.axis_index("ctx")
    e = lax.axis_index("exp")
    chip = c // 2
    core = lax.rem(c, 2)
    sibling = chip * 2 + 1 - core
    tok = query.shape[1]
    width = query.shape[2]
    half = out_proj.shape[0] // 2

    def chip_at(r):
        return lax.rem(chip + r, chips) * 2 + core

    def exp_at(r):
        return lax.rem(e + r, n_exp)

    barrier = pltpu.get_barrier_semaphore()
    for r in range(1, n_exp):
        pl.semaphore_signal(barrier, inc=1, device_id={"exp": exp_at(r)}, device_id_type=MESH)
    for r in range(1, chips):
        pl.semaphore_signal(barrier, inc=1, device_id={"ctx": chip_at(r)}, device_id_type=MESH)
    pl.semaphore_signal(barrier, inc=1, device_id={"ctx": sibling}, device_id_type=MESH)

    locals_ = [
        pltpu.make_async_copy(key.at[0], kbuf.at[c], local_sem.at[0]),
        pltpu.make_async_copy(value.at[0], vbuf.at[c], local_sem.at[1]),
        pltpu.make_async_copy(out_proj.at[pl.ds(0, half)], proj.at[e, 0], local_sem.at[2]),
        pltpu.make_async_copy(out_proj.at[pl.ds(half, half)], proj.at[e, 1], local_sem.at[3]),
        pltpu.make_async_copy(gate_up.at[0], gbuf.at[c], local_sem.at[4]),
        pltpu.make_async_copy(down.at[0], dbuf.at[c], local_sem.at[5]),
    ]
    for copy in locals_:
        copy.start()
    pl.semaphore_wait(barrier, n_exp - 1 + chips - 1 + 1)

    pending = []

    def remote(src, dst, send, recv, where):
        return pltpu.make_async_remote_copy(
            src_ref=src, dst_ref=dst, send_sem=send, recv_sem=recv, device_id=where, device_id_type=MESH
        )

    def spread(src, buf, send, recv):
        copies = []
        for r in range(1, chips):
            copies.append(remote(src, buf.at[c], send.at[r - 1], recv.at[c], {"ctx": chip_at(r)}))
        copies.append(remote(src, buf.at[c], send.at[chips - 1], recv.at[c], {"ctx": sibling}))
        for copy in copies:
            copy.start()
        return copies

    def landed(buf, send, recv, s):
        remote(buf.at[s], buf.at[s], send.at[0], recv.at[s], {"ctx": sibling}).wait_recv()

    def forward(buf, send, recv):
        for r in range(1, chips):
            s = chip_at(chips - r)
            landed(buf, send, recv, s)
            copy = remote(buf.at[s], buf.at[s], send.at[chips - 1 + r], recv.at[s], {"ctx": sibling})
            copy.start()
            pending.append(copy)

    def from_sibling(buf, send, recv):
        for r in range(chips):
            landed(buf, send, recv, lax.rem(chip + r, chips) * 2 + 1 - core)

    k_copies = spread(key.at[0], kbuf, k_send, k_recv)
    v_copies = spread(value.at[0], vbuf, v_send, v_recv)
    offsets = [0]
    for r in range(1, n_exp // 2 + 1):
        offsets.append(r)
        if n_exp - r != r:
            offsets.append(n_exp - r)
    own_half = out_proj.at[pl.ds(pl.multiple_of(core * half, half), half)]
    for r in reversed(offsets[1:]):
        copy = remote(own_half, proj.at[e, core], proj_send.at[r], proj_recv.at[e, core], {"exp": exp_at(r)})
        copy.start()
        pending.append(copy)

    forward(kbuf, k_send, k_recv)
    forward(vbuf, v_send, v_recv)
    for copy in k_copies + v_copies:
        copy.wait_send()
    pending.extend(spread(gate_up.at[0], gbuf, g_send, g_recv))
    pending.extend(spread(down.at[0], dbuf, d_send, d_recv))

    def proj_at(s, side):
        return remote(proj.at[s, side], proj.at[s, side], proj_fwd.at[s], proj_recv.at[s, side], {"ctx": sibling})

    for r in offsets[1:]:
        s = exp_at(r)
        proj_at(s, core).wait_recv()
        copy = proj_at(s, core)
        copy.start()
        pending.append(copy)

    for copy in locals_:
        copy.wait()
    from_sibling(kbuf, k_send, k_recv)
    from_sibling(vbuf, v_send, v_recv)

    keys = n_ctx * tok
    q_pos = c * tok + lax.broadcasted_iota(jnp.int32, (tok, keys), 0)
    k_pos = lax.broadcasted_iota(jnp.int32, (tok, keys), 1)
    allowed = k_pos <= q_pos
    for h in range(HEADS):
        cols = slice(h * HEAD_DIM, (h + 1) * HEAD_DIM)
        k_head = kbuf[:, :, cols].reshape(keys, HEAD_DIM)
        v_head = vbuf[:, :, cols].reshape(keys, HEAD_DIM)
        scores = lax.dot_general(
            query[0, :, cols], k_head, (((1,), (1,)), ((), ())), preferred_element_type=jnp.float32
        )
        scores = jnp.where(allowed, scores * (HEAD_DIM**-0.5), NEG_FILL)
        weights = jnp.exp(scores - jnp.max(scores, axis=1, keepdims=True))
        total = jnp.sum(weights, axis=1, keepdims=True)
        part = jnp.dot(weights.astype(jnp.bfloat16), v_head, preferred_element_type=jnp.float32)
        context[:, cols] = (part / total).astype(jnp.bfloat16)

    for r in offsets[1:]:
        proj_at(exp_at(r), 1 - core).wait_recv()
    attn_out = jnp.dot(
        context[...], proj[...].reshape(n_exp * 2 * half, width), preferred_element_type=jnp.float32
    )
    hidden = (residual[0].astype(jnp.float32) + attn_out).astype(jnp.bfloat16)
    wide = hidden.astype(jnp.float32)
    mean_square = jnp.mean(wide * wide, axis=1, keepdims=True)
    normed = (wide * lax.rsqrt(mean_square + 1e-06)).astype(jnp.bfloat16)

    ids = ids_ref[0]
    slots = []
    for k in range(2):
        away = ids[:, k : k + 1] - e
        away = jnp.where(away < 0, away + n_exp, away)
        slot = jnp.where(2 * away <= n_exp, 2 * away - 1, 2 * (n_exp - away))
        slots.append(jnp.where(away == 0, 0, slot))
    lane = lax.broadcasted_iota(jnp.int32, (tok, 128), 1)
    picks = [lane == slots[k] for k in range(2)]
    member = jnp.where(picks[0] | picks[1], 1.0, 0.0)
    below = jnp.where(
        lax.broadcasted_iota(jnp.int32, (tok, tok), 1) < lax.broadcasted_iota(jnp.int32, (tok, tok), 0), 1.0, 0.0
    ).astype(jnp.bfloat16)
    rank = jnp.dot(below, member.astype(jnp.bfloat16), preferred_element_type=jnp.float32)
    place = (member * (rank + 1.0)).astype(jnp.bfloat16)
    grid = (n_exp, cap, 128)
    rows = n_exp * cap
    spread_out = jnp.where(
        lax.broadcasted_iota(jnp.int32, grid, 0) == lax.broadcasted_iota(jnp.int32, grid, 2), 1.0, 0.0
    ).reshape(rows, 128)
    wanted = (lax.broadcasted_iota(jnp.int32, (n_exp, cap, tok), 1) + 1).astype(jnp.float32).reshape(rows, tok)
    held = lax.dot_general(
        spread_out.astype(jnp.bfloat16), place, (((1,), (1,)), ((), ())), preferred_element_type=jnp.float32
    )
    dispatch = jnp.where(held == wanted, 1.0, 0.0).astype(jnp.bfloat16)
    sent = jnp.dot(dispatch, normed, preferred_element_type=jnp.float32).astype(jnp.bfloat16)
    outgoing[...] = sent.reshape(n_exp, cap, width)
    for i in reversed(range(1, n_exp)):
        copy = remote(
            outgoing.at[i], arrived.at[i], out_send.at[i], out_recv.at[i], {"exp": exp_at(offsets[i])}
        )
        copy.start()
        pending.append(copy)
    arrived[0] = outgoing[0]

    affinity = jax.nn.sigmoid(jnp.dot(normed, router[...], preferred_element_type=jnp.float32))
    expert_lane = lax.broadcasted_iota(jnp.int32, affinity.shape, 1)
    picked = [
        jnp.sum(jnp.where(expert_lane == ids[:, k : k + 1], affinity, 0.0), axis=1, keepdims=True) for k in range(2)
    ]
    both = picked[0] + picked[1]
    column = lax.broadcasted_iota(jnp.int32, (tok, rows), 1).astype(jnp.float32)
    combine = jnp.zeros((tok, rows), jnp.float32)
    for k in range(2):
        own_rank = jnp.sum(jnp.where(picks[k], rank, 0.0), axis=1, keepdims=True)
        target = slots[k].astype(jnp.float32) * cap + own_rank
        combine = combine + jnp.where(column == target, picked[k] / both, 0.0)
    combine = combine.astype(jnp.bfloat16)

    forward(gbuf, g_send, g_recv)
    forward(dbuf, d_send, d_recv)
    from_sibling(gbuf, g_send, g_recv)
    from_sibling(dbuf, d_send, d_recv)

    ff = activation.shape[1]
    group = n_exp // 2
    chunk = 256
    for first in range(0, n_exp, group):
        for i in range(max(first, 1), first + group):
            remote(outgoing.at[i], arrived.at[i], out_send.at[i], out_recv.at[i], {"exp": exp_at(offsets[i])}).wait_recv()
        feats = arrived[first : first + group].reshape(group * cap, width)
        for f in range(0, ff, chunk):
            gate = jnp.dot(
                feats, gbuf[:, :, f : f + chunk].reshape(width, chunk), preferred_element_type=jnp.float32
            )
            up = jnp.dot(
                feats, gbuf[:, :, ff + f : ff + f + chunk].reshape(width, chunk), preferred_element_type=jnp.float32
            )
            activation[:, f : f + chunk] = (gate / (1.0 + jnp.exp(-gate)) * up).astype(jnp.bfloat16)
        made = jnp.dot(activation[...], dbuf[...].reshape(ff, width), preferred_element_type=jnp.float32)
        produced[first : first + group] = made.astype(jnp.bfloat16).reshape(group, cap, width)
        for i in reversed(range(max(first, 1), first + group)):
            copy = remote(
                produced.at[i],
                returned.at[i],
                back_send.at[i],
                back_recv.at[i],
                {"exp": exp_at(n_exp - offsets[i])},
            )
            copy.start()
            pending.append(copy)
    returned[0] = produced[0]
    for i in range(1, n_exp):
        remote(produced.at[i], returned.at[i], back_send.at[i], back_recv.at[i], {"exp": exp_at(offsets[i])}).wait_recv()
    moe = jnp.dot(combine, returned[...].reshape(rows, width), preferred_element_type=jnp.float32)
    out[0] = (wide + moe).astype(jnp.bfloat16)
    for copy in pending:
        copy.wait_send()


def on_device(
    residual, query_rows, key_rows, value_rows, out_proj, router, expert_ids, expert_gate_up, expert_down
):
    n_ctx = lax.axis_size("ctx")
    n_exp = lax.axis_size("exp")
    chips = n_ctx // 2
    _, tok, width = residual.shape
    cap = min(tok, -(-(3 * tok // n_exp) // 16) * 16)
    bf16 = jnp.bfloat16
    depth, twice_ff = expert_gate_up.shape[1:]
    ff_part = expert_down.shape[1]
    half = out_proj.shape[0] // 2
    vmem = pl.BlockSpec(memory_space=pltpu.VMEM)
    anywhere = pl.BlockSpec(memory_space=pl.ANY)
    dma = pltpu.SemaphoreType.DMA
    ctx_sems = [dma((2 * chips,)), dma((n_ctx,))]
    rows = n_exp * cap
    return pl.pallas_call(
        functools.partial(fused, n_ctx, n_exp, cap),
        out_shape=jax.ShapeDtypeStruct(residual.shape, bf16),
        in_specs=[vmem] * 4 + [anywhere] * 5,
        out_specs=vmem,
        scratch_shapes=[
            pltpu.VMEM((n_ctx, tok, width), bf16),
            pltpu.VMEM((n_ctx, tok, width), bf16),
            pltpu.VMEM((n_exp, 2, half, width), bf16),
            pltpu.VMEM((n_ctx, depth, twice_ff), bf16),
            pltpu.VMEM((n_ctx, ff_part, width), bf16),
            pltpu.VMEM((n_exp, cap, width), bf16),
            pltpu.VMEM((n_exp, cap, width), bf16),
            pltpu.VMEM((n_exp, cap, width), bf16),
            pltpu.VMEM((n_exp, cap, width), bf16),
            pltpu.VMEM((tok, width), bf16),
            pltpu.VMEM((rows // 2, twice_ff // 2), bf16),
            dma((6,)),
        ]
        + ctx_sems * 4
        + [dma((n_exp,)), dma((n_exp, 2)), dma((n_exp,))]
        + [dma((n_exp,))] * 4,
        compiler_params=pltpu.CompilerParams(
            collective_id=0, has_side_effects=True, vmem_limit_bytes=48 * 1024 * 1024
        ),
    )(residual, query_rows, router, expert_ids, key_rows, value_rows, out_proj, expert_gate_up, expert_down)


def solution(mesh):
    return jax.shard_map(
        on_device,
        mesh=mesh,
        in_specs=(
            P("exp", "ctx", None),
            P("exp", "ctx", None),
            P("exp", "ctx", None),
            P("exp", "ctx", None),
            P("exp", None),
            P(),
            P("exp", "ctx", None),
            P("exp", "ctx", None),
            P("exp", "ctx", None),
        ),
        out_specs=P("exp", "ctx", None),
        check_vma=False,
    )
```

time: 170 us -> 76.1 us (0.45)
  waiting for transfers between devices: 108 us -> 0 us
  Pallas kernels: 0 us -> 68.1 us
  starting transfers between devices: 19.2 us -> 0 us
  matrix products: 14.8 us -> 0 us
  between operations: 13.4 us -> 0.04 us
  other arithmetic: 6.39 us -> 0 us
    all_gather x4 -> x0, waiting for transfers between devices: 69.9 us -> none  [the longest x1 21.6 us: on_device(): lax.all_gather(expert_gate_up, 'ctx', axis=1, tiled=True)]
    pallas_call x0 -> x1, Pallas kernels: none -> 68.1 us  [on_device(): pl.pallas_call(functools.partial(fused, n_ctx, n_exp, cap), out_shape=jax...]
    all_to_all x5 -> x0, waiting for transfers between devices: 36.2 us -> none  [the longest x1 17.9 us: on_device(): lax.all_to_all(produced.reshape(arrived.shape), 'exp', split_axis=0, conc...]
    all_to_all x5 -> x0, starting transfers between devices: 19.1 us -> none  [the longest x1 5.52 us: on_device(): lax.all_to_all(produced.reshape(arrived.shape), 'exp', split_axis=0, conc...]
    dot_general x7 -> x0, matrix products: 14.8 us -> none  [the longest x1 4.74 us: on_device(): jnp.dot(flat_feats, full_gate_up[0], preferred_element_type=jnp.float32)]
    unnamed x14 -> x19, local copies, waits for them, and re-layouts: 2.07 us -> 7.63 us
    reduce_sum x6 -> x0, other arithmetic: 3.7 us -> none  [the longest x1 1.65 us: on_device(): moe_out = jnp.sum(gate_share[:, :, None] * pair_out, axis=1)]
    gather x6 -> x0, local copies, waits for them, and re-layouts: 3.15 us -> none  [the longest x4 1.79 us: on_device(): picked = jnp.take_along_axis(affinity, chosen_ids, axis=1)]
  transfers between devices with their start and end apart: 9 -> 0, of which waited for: 8 -> 0; matrix products, arithmetic and copies ran while one was open for 12% -> 0% of each run, Pallas kernels for 0% -> 0%
where the time goes in v1:
time: 76.1 us; the launch traced here: 75.7 us
  Pallas kernels  68.1 us (89%)
  local copies, waits for them, and re-layouts  7.63 us (10%)
    pallas_call x1, Pallas kernels, on_device(): pl.pallas_call(functools.partial(fused, n_ctx, n_exp, cap), out_shape=jax...  68.1 us
    unnamed x19, local copies, waits for them, and re-layouts  7.63 us

profile of v1, /device:TPU:0, one launch (start us, length us, event | category | flops | bytes accessed | tf_op | source)
XLA Modules:
  0.0 75.7 jit_solution(13392559969139946776)
XLA Ops:
  0.0 0.0 copy-start.7
  0.0 0.0 copy-start.2
  0.0 0.8 %copy.11.ids_ref = s32[1,128,2]{2,1,0:T(8,128)S(1)} copy(s32[1,128,2]{1,2,0:T(2,128)} %param.15) | data formatting | bytes 2048 | tf_op args[6]
  0.8 0.0 copy-done.7
  0.8 0.2 copy.10.router
  1.0 0.0 copy-done.2
  1.0 0.0 copy-start
  1.0 1.1 %copy-done = bf16[1,256,1536]{2,1,0:T(8,128)(2,1)S(1)} copy-done((bf16[1,256,1536]{2,1,0:T(8,128)(2,1)S(1)}, bf16[1,256,1536]{2,1,0:T(8,128)(2,1)}, u32[]{:S(2)}) %copy-start) | copy-done | bytes 786456
  2.2 0.0 copy-start.1
  2.2 1.0 %copy-done.1 = bf16[1,192,1024]{2,1,0:T(8,128)(2,1)S(1)} copy-done((bf16[1,192,1024]{2,1,0:T(8,128)(2,1)S(1)}, bf16[1,192,1024]{2,1,0:T(8,128)(2,1)}, u32[]{:S(2)}) %copy-start.1) | copy-done | bytes 393240
  3.2 0.0 copy-start.3
  3.2 0.9 %copy-done.3 = bf16[1,128,1024]{2,1,0:T(8,128)(2,1)S(1)} copy-done((bf16[1,128,1024]{2,1,0:T(8,128)(2,1)S(1)}, bf16[1,128,1024]{2,1,0:T(8,128)(2,1)}, u32[]{:S(2)}) %copy-start.3) | copy-done | bytes 262168
  4.1 0.0 copy-start.4
  4.1 0.9 %copy-done.4 = bf16[1,128,1024]{2,1,0:T(8,128)(2,1)S(1)} copy-done((bf16[1,128,1024]{2,1,0:T(8,128)(2,1)S(1)}, bf16[1,128,1024]{2,1,0:T(8,128)(2,1)}, u32[]{:S(2)}) %copy-start.4) | copy-done | bytes 262168
  5.1 0.0 copy-start.5
  5.1 0.9 %copy-done.5 = bf16[1,128,1024]{2,1,0:T(8,128)(2,1)S(1)} copy-done((bf16[1,128,1024]{2,1,0:T(8,128)(2,1)S(1)}, bf16[1,128,1024]{2,1,0:T(8,128)(2,1)}, u32[]{:S(2)}) %copy-start.5) | copy-done | bytes 262168
  6.0 0.0 copy-start.6
  6.0 0.9 %copy-done.6 = bf16[128,1024]{1,0:T(8,128)(2,1)S(1)} copy-done((bf16[128,1024]{1,0:T(8,128)(2,1)S(1)}, bf16[128,1024]{1,0:T(8,128)(2,1)}, u32[]{:S(2)}) %copy-start.6) | copy-done | bytes 262168
  7.0 68.1 %shard_map.91 = bf16[1,128,1024]{2,1,0:T(8,128)(2,1)S(1)} custom-call(bf16[1,128,1024]{2,1,0:T(8,128)(2,1)S(1)} %copy-done.2, bf16[1,128,1024]{2,1,0:T(8,128)(2,1)S(1)} %copy-done.3, bf16[1024,8]{1,0:T(8,128)(2,1)S(1)} %copy.10.router, s32[1,128,2]{2,1,0:T(8,128)S(1)} %copy.11.ids_ref, bf16[1,128,1024]{2,1,0:T(8,128)(2,1)S(1)} %copy-done.4, ...), custom_call_target="tpu_custom_call" | custom-call | tf_op jit(solution)/shard_map/pallas_call | solution.py:293
  75.0 0.7 copy.13
Async XLA Ops:
  0.0 0.8 %copy-start.7 = (bf16[1024,8]{0,1:T(8,128)(2,1)S(1)}, bf16[1024,8]{0,1:T(8,128)(2,1)}, u32[]{:S(2)}) copy-start(bf16[1024,8]{0,1:T(8,128)(2,1)} %param.14) | copy-start | bytes 49156
  0.0 1.0 %copy-start.2 = (bf16[1,128,1024]{2,1,0:T(8,128)(2,1)S(1)}, bf16[1,128,1024]{2,1,0:T(8,128)(2,1)}, u32[]{:S(2)}) copy-start(bf16[1,128,1024]{2,1,0:T(8,128)(2,1)} %residual.1) | copy-start | bytes 786436
  1.0 1.1 %copy-start = (bf16[1,256,1536]{2,1,0:T(8,128)(2,1)S(1)}, bf16[1,256,1536]{2,1,0:T(8,128)(2,1)}, u32[]{:S(2)}) copy-start(bf16[1,256,1536]{2,1,0:T(8,128)(2,1)} %gate_up.1) | copy-start | bytes 2359300
  2.2 1.0 %copy-start.1 = (bf16[1,192,1024]{2,1,0:T(8,128)(2,1)S(1)}, bf16[1,192,1024]{2,1,0:T(8,128)(2,1)}, u32[]{:S(2)}) copy-start(bf16[1,192,1024]{2,1,0:T(8,128)(2,1)} %down.1) | copy-start | bytes 1179652
  3.2 0.9 %copy-start.3 = (bf16[1,128,1024]{2,1,0:T(8,128)(2,1)S(1)}, bf16[1,128,1024]{2,1,0:T(8,128)(2,1)}, u32[]{:S(2)}) copy-start(bf16[1,128,1024]{2,1,0:T(8,128)(2,1)} %query.1) | copy-start | bytes 786436
  4.1 0.9 %copy-start.4 = (bf16[1,128,1024]{2,1,0:T(8,128)(2,1)S(1)}, bf16[1,128,1024]{2,1,0:T(8,128)(2,1)}, u32[]{:S(2)}) copy-start(bf16[1,128,1024]{2,1,0:T(8,128)(2,1)} %key.1) | copy-start | bytes 786436
  5.1 0.9 %copy-start.5 = (bf16[1,128,1024]{2,1,0:T(8,128)(2,1)S(1)}, bf16[1,128,1024]{2,1,0:T(8,128)(2,1)}, u32[]{:S(2)}) copy-start(bf16[1,128,1024]{2,1,0:T(8,128)(2,1)} %value.1) | copy-start | bytes 786436
  6.0 0.9 %copy-start.6 = (bf16[128,1024]{1,0:T(8,128)(2,1)S(1)}, bf16[128,1024]{1,0:T(8,128)(2,1)}, u32[]{:S(2)}) copy-start(bf16[128,1024]{1,0:T(8,128)(2,1)} %out_proj.1) | copy-start | bytes 786436

commit v2 on v1

--- a/solution.py
+++ b/solution.py
@@ -17,18 +17,21 @@
     n_ctx,
     n_exp,
     cap,
-    residual,
-    query,
-    router,
-    ids_ref,
+    residual_in,
+    query_in,
+    router_in,
+    ids_in,
     key,
     value,
     out_proj,
     gate_up,
     down,
     out,
-    kbuf,
-    vbuf,
+    residual,
+    query,
+    router,
+    ids_ref,
+    kvbuf,
     proj,
     gbuf,
     dbuf,
@@ -39,10 +42,9 @@
     context,
     activation,
     local_sem,
-    k_send,
-    k_recv,
-    v_send,
-    v_recv,
+    kv_local,
+    kv_send,
+    kv_recv,
     g_send,
     g_recv,
     d_send,
@@ -61,8 +63,9 @@
     chip = c // 2
     core = lax.rem(c, 2)
     sibling = chip * 2 + 1 - core
-    tok = query.shape[1]
-    width = query.shape[2]
+    tok, width = query.shape
+    groups = kvbuf.shape[1] // 2
+    group_cols = kvbuf.shape[3]
     half = out_proj.shape[0] // 2
 
     def chip_at(r):
@@ -79,13 +82,21 @@
     pl.semaphore_signal(barrier, inc=1, device_id={"ctx": sibling}, device_id_type=MESH)
 
     locals_ = [
-        pltpu.make_async_copy(key.at[0], kbuf.at[c], local_sem.at[0]),
-        pltpu.make_async_copy(value.at[0], vbuf.at[c], local_sem.at[1]),
+        pltpu.make_async_copy(query_in.at[0], query, local_sem.at[0]),
+        pltpu.make_async_copy(residual_in.at[0], residual, local_sem.at[1]),
         pltpu.make_async_copy(out_proj.at[pl.ds(0, half)], proj.at[e, 0], local_sem.at[2]),
         pltpu.make_async_copy(out_proj.at[pl.ds(half, half)], proj.at[e, 1], local_sem.at[3]),
         pltpu.make_async_copy(gate_up.at[0], gbuf.at[c], local_sem.at[4]),
         pltpu.make_async_copy(down.at[0], dbuf.at[c], local_sem.at[5]),
+        pltpu.make_async_copy(router_in, router, local_sem.at[6]),
+        pltpu.make_async_copy(ids_in.at[0], ids_ref, local_sem.at[7]),
     ]
+    kv_parts = []
+    for g in range(groups):
+        for ref in (key, value):
+            kv_parts.append(ref.at[0, :, pl.ds(g * group_cols, group_cols)])
+    for i, part in enumerate(kv_parts):
+        locals_.append(pltpu.make_async_copy(part, kvbuf.at[c, i], kv_local.at[i]))
     for copy in locals_:
         copy.start()
     pl.semaphore_wait(barrier, n_exp - 1 + chips - 1 + 1)
@@ -121,8 +132,10 @@
         for r in range(chips):
             landed(buf, send, recv, lax.rem(chip + r, chips) * 2 + 1 - core)
 
-    k_copies = spread(key.at[0], kbuf, k_send, k_recv)
-    v_copies = spread(value.at[0], vbuf, v_send, v_recv)
+    kv_copies = []
+    kv_views = [(kvbuf.at[:, i], kv_send.at[i], kv_recv.at[i]) for i in range(2 * groups)]
+    for part, view in zip(kv_parts, kv_views):
+        kv_copies += spread(part, *view)
     offsets = [0]
     for r in range(1, n_exp // 2 + 1):
         offsets.append(r)
@@ -134,56 +147,64 @@
         copy.start()
         pending.append(copy)
 
-    forward(kbuf, k_send, k_recv)
-    forward(vbuf, v_send, v_recv)
-    for copy in k_copies + v_copies:
-        copy.wait_send()
-    pending.extend(spread(gate_up.at[0], gbuf, g_send, g_recv))
-    pending.extend(spread(down.at[0], dbuf, d_send, d_recv))
-
     def proj_at(s, side):
         return remote(proj.at[s, side], proj.at[s, side], proj_fwd.at[s], proj_recv.at[s, side], {"ctx": sibling})
 
-    for r in offsets[1:]:
-        s = exp_at(r)
-        proj_at(s, core).wait_recv()
-        copy = proj_at(s, core)
-        copy.start()
-        pending.append(copy)
-
     for copy in locals_:
         copy.wait()
-    from_sibling(kbuf, k_send, k_recv)
-    from_sibling(vbuf, v_send, v_recv)
-
     keys = n_ctx * tok
     q_pos = c * tok + lax.broadcasted_iota(jnp.int32, (tok, keys), 0)
     k_pos = lax.broadcasted_iota(jnp.int32, (tok, keys), 1)
     allowed = k_pos <= q_pos
-    for h in range(HEADS):
-        cols = slice(h * HEAD_DIM, (h + 1) * HEAD_DIM)
-        k_head = kbuf[:, :, cols].reshape(keys, HEAD_DIM)
-        v_head = vbuf[:, :, cols].reshape(keys, HEAD_DIM)
-        scores = lax.dot_general(
-            query[0, :, cols], k_head, (((1,), (1,)), ((), ())), preferred_element_type=jnp.float32
-        )
-        scores = jnp.where(allowed, scores * (HEAD_DIM**-0.5), NEG_FILL)
-        weights = jnp.exp(scores - jnp.max(scores, axis=1, keepdims=True))
-        total = jnp.sum(weights, axis=1, keepdims=True)
-        part = jnp.dot(weights.astype(jnp.bfloat16), v_head, preferred_element_type=jnp.float32)
-        context[:, cols] = (part / total).astype(jnp.bfloat16)
+    for g in range(groups):
+        forward(*kv_views[2 * g])
+        forward(*kv_views[2 * g + 1])
+        if g == groups - 1:
+            for copy in kv_copies:
+                copy.wait_send()
+            pending.extend(spread(gate_up.at[0], gbuf, g_send, g_recv))
+            pending.extend(spread(down.at[0], dbuf, d_send, d_recv))
+            for r in offsets[1:]:
+                s = exp_at(r)
+                proj_at(s, core).wait_recv()
+                copy = proj_at(s, core)
+                copy.start()
+                pending.append(copy)
+        from_sibling(*kv_views[2 * g])
+        from_sibling(*kv_views[2 * g + 1])
+        for h in range(group_cols // HEAD_DIM):
+            inner = slice(h * HEAD_DIM, (h + 1) * HEAD_DIM)
+            cols = slice(g * group_cols + h * HEAD_DIM, g * group_cols + (h + 1) * HEAD_DIM)
+            k_head = kvbuf[:, 2 * g, :, inner].reshape(keys, HEAD_DIM)
+            v_head = kvbuf[:, 2 * g + 1, :, inner].reshape(keys, HEAD_DIM)
+            scores = lax.dot_general(
+                query[:, cols], k_head, (((1,), (1,)), ((), ())), preferred_element_type=jnp.float32
+            )
+            scores = jnp.where(allowed, scores * (HEAD_DIM**-0.5), NEG_FILL)
+            weights = jnp.exp(scores - jnp.max(scores, axis=1, keepdims=True))
+            total = jnp.sum(weights, axis=1, keepdims=True)
+            part = jnp.dot(weights.astype(jnp.bfloat16), v_head, preferred_element_type=jnp.float32)
+            context[:, cols] = (part / total).astype(jnp.bfloat16)
 
     for r in offsets[1:]:
         proj_at(exp_at(r), 1 - core).wait_recv()
     attn_out = jnp.dot(
         context[...], proj[...].reshape(n_exp * 2 * half, width), preferred_element_type=jnp.float32
     )
-    hidden = (residual[0].astype(jnp.float32) + attn_out).astype(jnp.bfloat16)
+    hidden = (residual[...].astype(jnp.float32) + attn_out).astype(jnp.bfloat16)
     wide = hidden.astype(jnp.float32)
     mean_square = jnp.mean(wide * wide, axis=1, keepdims=True)
     normed = (wide * lax.rsqrt(mean_square + 1e-06)).astype(jnp.bfloat16)
 
-    ids = ids_ref[0]
+    eye = jnp.where(
+        lax.broadcasted_iota(jnp.int32, (tok, tok), 1) == lax.broadcasted_iota(jnp.int32, (tok, tok), 0), 1.0, 0.0
+    ).astype(jnp.bfloat16)
+    ids = lax.dot_general(
+        eye,
+        ids_ref[...].astype(jnp.float32).astype(jnp.bfloat16),
+        (((1,), (1,)), ((), ())),
+        preferred_element_type=jnp.float32,
+    ).astype(jnp.int32)
     slots = []
     for k in range(2):
         away = ids[:, k : k + 1] - e
@@ -218,7 +239,9 @@
         pending.append(copy)
     arrived[0] = outgoing[0]
 
-    affinity = jax.nn.sigmoid(jnp.dot(normed, router[...], preferred_element_type=jnp.float32))
+    affinity = jax.nn.sigmoid(
+        lax.dot_general(normed, router[...], (((1,), (1,)), ((), ())), preferred_element_type=jnp.float32)
+    )
     expert_lane = lax.broadcasted_iota(jnp.int32, affinity.shape, 1)
     picked = [
         jnp.sum(jnp.where(expert_lane == ids[:, k : k + 1], affinity, 0.0), axis=1, keepdims=True) for k in range(2)
@@ -233,16 +256,15 @@
     combine = combine.astype(jnp.bfloat16)
 
     forward(gbuf, g_send, g_recv)
-    forward(dbuf, d_send, d_recv)
     from_sibling(gbuf, g_send, g_recv)
-    from_sibling(dbuf, d_send, d_recv)
-
     ff = activation.shape[1]
     group = n_exp // 2
     chunk = 256
     for first in range(0, n_exp, group):
         for i in range(max(first, 1), first + group):
-            remote(outgoing.at[i], arrived.at[i], out_send.at[i], out_recv.at[i], {"exp": exp_at(offsets[i])}).wait_recv()
+            remote(
+                outgoing.at[i], arrived.at[i], out_send.at[i], out_recv.at[i], {"exp": exp_at(offsets[i])}
+            ).wait_recv()
         feats = arrived[first : first + group].reshape(group * cap, width)
         for f in range(0, ff, chunk):
             gate = jnp.dot(
@@ -251,8 +273,17 @@
             up = jnp.dot(
                 feats, gbuf[:, :, ff + f : ff + f + chunk].reshape(width, chunk), preferred_element_type=jnp.float32
             )
-            activation[:, f : f + chunk] = (gate / (1.0 + jnp.exp(-gate)) * up).astype(jnp.bfloat16)
-        made = jnp.dot(activation[...], dbuf[...].reshape(ff, width), preferred_element_type=jnp.float32)
+            activation[first * cap : (first + group) * cap, f : f + chunk] = (
+                gate / (1.0 + jnp.exp(-gate)) * up
+            ).astype(jnp.bfloat16)
+    forward(dbuf, d_send, d_recv)
+    from_sibling(dbuf, d_send, d_recv)
+    for first in (group, 0):
+        made = jnp.dot(
+            activation[first * cap : (first + group) * cap],
+            dbuf[...].reshape(ff, width),
+            preferred_element_type=jnp.float32,
+        )
         produced[first : first + group] = made.astype(jnp.bfloat16).reshape(group, cap, width)
         for i in reversed(range(max(first, 1), first + group)):
             copy = remote(
@@ -290,14 +321,18 @@
     dma = pltpu.SemaphoreType.DMA
     ctx_sems = [dma((2 * chips,)), dma((n_ctx,))]
     rows = n_exp * cap
+    groups = 4
     return pl.pallas_call(
         functools.partial(fused, n_ctx, n_exp, cap),
         out_shape=jax.ShapeDtypeStruct(residual.shape, bf16),
-        in_specs=[vmem] * 4 + [anywhere] * 5,
+        in_specs=[anywhere] * 9,
         out_specs=vmem,
         scratch_shapes=[
-            pltpu.VMEM((n_ctx, tok, width), bf16),
-            pltpu.VMEM((n_ctx, tok, width), bf16),
+            pltpu.VMEM((tok, width), bf16),
+            pltpu.VMEM((tok, width), bf16),
+            pltpu.VMEM((n_exp, width), bf16),
+            pltpu.VMEM((2, tok), jnp.int32),
+            pltpu.VMEM((n_ctx, 2 * groups, tok, width // groups), bf16),
             pltpu.VMEM((n_exp, 2, half, width), bf16),
             pltpu.VMEM((n_ctx, depth, twice_ff), bf16),
             pltpu.VMEM((n_ctx, ff_part, width), bf16),
@@ -306,16 +341,29 @@
             pltpu.VMEM((n_exp, cap, width), bf16),
             pltpu.VMEM((n_exp, cap, width), bf16),
             pltpu.VMEM((tok, width), bf16),
-            pltpu.VMEM((rows // 2, twice_ff // 2), bf16),
-            dma((6,)),
+            pltpu.VMEM((rows, twice_ff // 2), bf16),
+            dma((8,)),
+            dma((2 * groups,)),
+            dma((2 * groups, 2 * chips)),
+            dma((2 * groups, n_ctx)),
         ]
-        + ctx_sems * 4
+        + ctx_sems * 2
         + [dma((n_exp,)), dma((n_exp, 2)), dma((n_exp,))]
         + [dma((n_exp,))] * 4,
         compiler_params=pltpu.CompilerParams(
-            collective_id=0, has_side_effects=True, vmem_limit_bytes=48 * 1024 * 1024
+            collective_id=0, has_side_effects=True, vmem_limit_bytes=60 * 1024 * 1024
         ),
-    )(residual, query_rows, router, expert_ids, key_rows, value_rows, out_proj, expert_gate_up, expert_down)
+    )(
+        residual,
+        query_rows,
+        router.T,
+        jnp.swapaxes(expert_ids, 1, 2),
+        key_rows,
+        value_rows,
+        out_proj,
+        expert_gate_up,
+        expert_down,
+    )
 
 
 def solution(mesh):

time: 76.1 us -> 71.4 us (0.938)
  local copies, waits for them, and re-layouts: 7.63 us -> 1.67 us
    unnamed x19 -> x1, local copies, waits for them, and re-layouts: 7.63 us -> 1.67 us
where the time goes in v2:
time: 71.4 us; the launch traced here: 70.4 us
  Pallas kernels  68.7 us (96%)
  local copies, waits for them, and re-layouts  1.67 us (2%)
    pallas_call x1, Pallas kernels, on_device(): pl.pallas_call(functools.partial(fused, n_ctx, n_exp, cap), out_shape=jax...  68.7 us
    unnamed x1, local copies, waits for them, and re-layouts  1.67 us

profile of v2, /device:TPU:0, one launch (start us, length us, event | category | flops | bytes accessed | tf_op | source)
XLA Modules:
  0.0 70.4 jit_solution(17700170471646483373)
XLA Ops:
  0.0 68.7 %shard_map.91 = bf16[1,128,1024]{2,1,0:T(8,128)(2,1)} custom-call(bf16[1,128,1024]{2,1,0:T(8,128)(2,1)} %residual_in.1, bf16[1,128,1024]{2,1,0:T(8,128)(2,1)} %query_in.1, bf16[8,1024]{1,0:T(8,128)(2,1)} %bitcast.2, s32[1,2,128]{2,1,0:T(2,128)} %bitcast.3, bf16[1,128,1024]{2,1,0:T(8,128)(2,1)} %key.1, bf16[1,128,1024]{2,1,0:T(8,128)(2,1)} %value.1, ...), custom_call_target="tpu_custom_call" | custom-call | tf_op jit(solution)/shard_map/pallas_call | solution.py:325
  68.8 1.7 %copy.11 = bf16[1,128,1024]{2,1,0:T(8,128)(2,1)} copy(bf16[1,128,1024]{2,1,0:T(8,128)(2,1)} %shard_map.91) | data formatting | bytes 524288

commit v3 on v2

--- a/solution.py
+++ b/solution.py
@@ -67,6 +67,7 @@
     groups = kvbuf.shape[1] // 2
     group_cols = kvbuf.shape[3]
     half = out_proj.shape[0] // 2
+    part_depth = gbuf.shape[2]
 
     def chip_at(r):
         return lax.rem(chip + r, chips) * 2 + core
@@ -86,7 +87,8 @@
         pltpu.make_async_copy(residual_in.at[0], residual, local_sem.at[1]),
         pltpu.make_async_copy(out_proj.at[pl.ds(0, half)], proj.at[e, 0], local_sem.at[2]),
         pltpu.make_async_copy(out_proj.at[pl.ds(half, half)], proj.at[e, 1], local_sem.at[3]),
-        pltpu.make_async_copy(gate_up.at[0], gbuf.at[c], local_sem.at[4]),
+        pltpu.make_async_copy(gate_up.at[0, pl.ds(0, part_depth)], gbuf.at[c, 0], local_sem.at[4]),
+        pltpu.make_async_copy(gate_up.at[0, pl.ds(part_depth, part_depth)], gbuf.at[c, 1], local_sem.at[8]),
         pltpu.make_async_copy(down.at[0], dbuf.at[c], local_sem.at[5]),
         pltpu.make_async_copy(router_in, router, local_sem.at[6]),
         pltpu.make_async_copy(ids_in.at[0], ids_ref, local_sem.at[7]),
@@ -132,10 +134,14 @@
         for r in range(chips):
             landed(buf, send, recv, lax.rem(chip + r, chips) * 2 + 1 - core)
 
-    kv_copies = []
+    kv_copies = {}
     kv_views = [(kvbuf.at[:, i], kv_send.at[i], kv_recv.at[i]) for i in range(2 * groups)]
-    for part, view in zip(kv_parts, kv_views):
-        kv_copies += spread(part, *view)
+
+    def send_group(g):
+        kv_copies[g] = spread(kv_parts[2 * g], *kv_views[2 * g]) + spread(kv_parts[2 * g + 1], *kv_views[2 * g + 1])
+
+    send_group(0)
+    send_group(1)
     offsets = [0]
     for r in range(1, n_exp // 2 + 1):
         offsets.append(r)
@@ -147,6 +153,9 @@
         copy.start()
         pending.append(copy)
 
+    gate_parts = [gate_up.at[0, pl.ds(i * part_depth, part_depth)] for i in range(2)]
+    gate_views = [(gbuf.at[:, i], g_send.at[i], g_recv.at[i]) for i in range(2)]
+
     def proj_at(s, side):
         return remote(proj.at[s, side], proj.at[s, side], proj_fwd.at[s], proj_recv.at[s, side], {"ctx": sibling})
 
@@ -159,11 +168,14 @@
     for g in range(groups):
         forward(*kv_views[2 * g])
         forward(*kv_views[2 * g + 1])
+        for copy in kv_copies[g]:
+            copy.wait_send()
+        if g + 2 < groups:
+            send_group(g + 2)
+        if g == groups - 2:
+            first_half = spread(gate_parts[0], *gate_views[0])
         if g == groups - 1:
-            for copy in kv_copies:
-                copy.wait_send()
-            pending.extend(spread(gate_up.at[0], gbuf, g_send, g_recv))
-            pending.extend(spread(down.at[0], dbuf, d_send, d_recv))
+            pending.extend(spread(gate_parts[1], *gate_views[1]))
             for r in offsets[1:]:
                 s = exp_at(r)
                 proj_at(s, core).wait_recv()
@@ -255,8 +267,13 @@
         combine = combine + jnp.where(column == target, picked[k] / both, 0.0)
     combine = combine.astype(jnp.bfloat16)
 
-    forward(gbuf, g_send, g_recv)
-    from_sibling(gbuf, g_send, g_recv)
+    for copy in first_half:
+        copy.wait_send()
+    forward(*gate_views[0])
+    pending.extend(spread(down.at[0], dbuf, d_send, d_recv))
+    forward(*gate_views[1])
+    from_sibling(*gate_views[0])
+    from_sibling(*gate_views[1])
     ff = activation.shape[1]
     group = n_exp // 2
     chunk = 256
@@ -268,10 +285,10 @@
         feats = arrived[first : first + group].reshape(group * cap, width)
         for f in range(0, ff, chunk):
             gate = jnp.dot(
-                feats, gbuf[:, :, f : f + chunk].reshape(width, chunk), preferred_element_type=jnp.float32
+                feats, gbuf[:, :, :, f : f + chunk].reshape(width, chunk), preferred_element_type=jnp.float32
             )
             up = jnp.dot(
-                feats, gbuf[:, :, ff + f : ff + f + chunk].reshape(width, chunk), preferred_element_type=jnp.float32
+                feats, gbuf[:, :, :, ff + f : ff + f + chunk].reshape(width, chunk), preferred_element_type=jnp.float32
             )
             activation[first * cap : (first + group) * cap, f : f + chunk] = (
                 gate / (1.0 + jnp.exp(-gate)) * up
@@ -334,7 +351,7 @@
             pltpu.VMEM((2, tok), jnp.int32),
             pltpu.VMEM((n_ctx, 2 * groups, tok, width // groups), bf16),
             pltpu.VMEM((n_exp, 2, half, width), bf16),
-            pltpu.VMEM((n_ctx, depth, twice_ff), bf16),
+            pltpu.VMEM((n_ctx, 2, depth // 2, twice_ff), bf16),
             pltpu.VMEM((n_ctx, ff_part, width), bf16),
             pltpu.VMEM((n_exp, cap, width), bf16),
             pltpu.VMEM((n_exp, cap, width), bf16),
@@ -342,12 +359,13 @@
             pltpu.VMEM((n_exp, cap, width), bf16),
             pltpu.VMEM((tok, width), bf16),
             pltpu.VMEM((rows, twice_ff // 2), bf16),
-            dma((8,)),
+            dma((9,)),
             dma((2 * groups,)),
             dma((2 * groups, 2 * chips)),
             dma((2 * groups, n_ctx)),
         ]
-        + ctx_sems * 2
+        + [dma((2, 2 * chips)), dma((2, n_ctx))]
+        + ctx_sems
         + [dma((n_exp,)), dma((n_exp, 2)), dma((n_exp,))]
         + [dma((n_exp,))] * 4,
         compiler_params=pltpu.CompilerParams(

time: 71.4 us -> 71.5 us (level)
  no operation moved by 1% of the time
where the time goes in v3:
time: 71.5 us; the launch traced here: 70.5 us
  Pallas kernels  68.8 us (96%)
  local copies, waits for them, and re-layouts  1.67 us (2%)
    pallas_call x1, Pallas kernels, on_device(): pl.pallas_call(functools.partial(fused, n_ctx, n_exp, cap), out_shape=jax...  68.8 us
    unnamed x1, local copies, waits for them, and re-layouts  1.67 us

profile of v3, /device:TPU:0, one launch (start us, length us, event | category | flops | bytes accessed | tf_op | source)
XLA Modules:
  0.0 70.5 jit_solution(10008596779866830598)
XLA Ops:
  0.0 68.8 %shard_map.91 = bf16[1,128,1024]{2,1,0:T(8,128)(2,1)} custom-call(bf16[1,128,1024]{2,1,0:T(8,128)(2,1)} %residual_in.1, bf16[1,128,1024]{2,1,0:T(8,128)(2,1)} %query_in.1, bf16[8,1024]{1,0:T(8,128)(2,1)} %bitcast.2, s32[1,2,128]{2,1,0:T(2,128)} %bitcast.3, bf16[1,128,1024]{2,1,0:T(8,128)(2,1)} %key.1, bf16[1,128,1024]{2,1,0:T(8,128)(2,1)} %value.1, ...), custom_call_target="tpu_custom_call" | custom-call | tf_op jit(solution)/shard_map/pallas_call | solution.py:342
  68.8 1.7 %copy.11 = bf16[1,128,1024]{2,1,0:T(8,128)(2,1)} copy(bf16[1,128,1024]{2,1,0:T(8,128)(2,1)} %shard_map.91) | data formatting | bytes 524288

commit v4 on v3

--- a/solution.py
+++ b/solution.py
@@ -26,7 +26,9 @@
     out_proj,
     gate_up,
     down,
-    out,
+    returned,
+    hidden_out,
+    combine_out,
     residual,
     query,
     router,
@@ -38,7 +40,10 @@
     outgoing,
     arrived,
     produced,
-    returned,
+    dispatch,
+    chosen,
+    hidden_part,
+    combine_part,
     context,
     activation,
     local_sem,
@@ -161,6 +166,46 @@
 
     for copy in locals_:
         copy.wait()
+
+    eye = jnp.where(
+        lax.broadcasted_iota(jnp.int32, (tok, tok), 1) == lax.broadcasted_iota(jnp.int32, (tok, tok), 0), 1.0, 0.0
+    ).astype(jnp.bfloat16)
+    ids = lax.dot_general(
+        eye,
+        ids_ref[...].astype(jnp.float32).astype(jnp.bfloat16),
+        (((1,), (1,)), ((), ())),
+        preferred_element_type=jnp.float32,
+    ).astype(jnp.int32)
+    slots = []
+    for k in range(2):
+        away = ids[:, k : k + 1] - e
+        away = jnp.where(away < 0, away + n_exp, away)
+        slot = jnp.where(2 * away <= n_exp, 2 * away - 1, 2 * (n_exp - away))
+        slots.append(jnp.where(away == 0, 0, slot))
+    lane = lax.broadcasted_iota(jnp.int32, (tok, 128), 1)
+    picks = [lane == slots[k] for k in range(2)]
+    member = jnp.where(picks[0] | picks[1], 1.0, 0.0)
+    below = jnp.where(
+        lax.broadcasted_iota(jnp.int32, (tok, tok), 1) < lax.broadcasted_iota(jnp.int32, (tok, tok), 0), 1.0, 0.0
+    ).astype(jnp.bfloat16)
+    rank = jnp.dot(below, member.astype(jnp.bfloat16), preferred_element_type=jnp.float32)
+    place = (member * (rank + 1.0)).astype(jnp.bfloat16)
+    grid = (n_exp, cap, 128)
+    rows = n_exp * cap
+    spread_out = jnp.where(
+        lax.broadcasted_iota(jnp.int32, grid, 0) == lax.broadcasted_iota(jnp.int32, grid, 2), 1.0, 0.0
+    ).reshape(rows, 128)
+    wanted = (lax.broadcasted_iota(jnp.int32, (n_exp, cap, tok), 1) + 1).astype(jnp.float32).reshape(rows, tok)
+    held = lax.dot_general(
+        spread_out.astype(jnp.bfloat16), place, (((1,), (1,)), ((), ())), preferred_element_type=jnp.float32
+    )
+    dispatch[...] = jnp.where(held == wanted, 1.0, 0.0).astype(jnp.bfloat16)
+    column = lax.broadcasted_iota(jnp.int32, (tok, rows), 1).astype(jnp.float32)
+    for k in range(2):
+        own_rank = jnp.sum(jnp.where(picks[k], rank, 0.0), axis=1, keepdims=True)
+        target = slots[k].astype(jnp.float32) * cap + own_rank
+        chosen[k] = jnp.where(column == target, 1.0, 0.0)
+
     keys = n_ctx * tok
     q_pos = c * tok + lax.broadcasted_iota(jnp.int32, (tok, keys), 0)
     k_pos = lax.broadcasted_iota(jnp.int32, (tok, keys), 1)
@@ -204,51 +249,23 @@
         context[...], proj[...].reshape(n_exp * 2 * half, width), preferred_element_type=jnp.float32
     )
     hidden = (residual[...].astype(jnp.float32) + attn_out).astype(jnp.bfloat16)
+    hidden_part[...] = hidden
     wide = hidden.astype(jnp.float32)
     mean_square = jnp.mean(wide * wide, axis=1, keepdims=True)
     normed = (wide * lax.rsqrt(mean_square + 1e-06)).astype(jnp.bfloat16)
 
-    eye = jnp.where(
-        lax.broadcasted_iota(jnp.int32, (tok, tok), 1) == lax.broadcasted_iota(jnp.int32, (tok, tok), 0), 1.0, 0.0
-    ).astype(jnp.bfloat16)
-    ids = lax.dot_general(
-        eye,
-        ids_ref[...].astype(jnp.float32).astype(jnp.bfloat16),
-        (((1,), (1,)), ((), ())),
-        preferred_element_type=jnp.float32,
-    ).astype(jnp.int32)
-    slots = []
-    for k in range(2):
-        away = ids[:, k : k + 1] - e
-        away = jnp.where(away < 0, away + n_exp, away)
-        slot = jnp.where(2 * away <= n_exp, 2 * away - 1, 2 * (n_exp - away))
-        slots.append(jnp.where(away == 0, 0, slot))
-    lane = lax.broadcasted_iota(jnp.int32, (tok, 128), 1)
-    picks = [lane == slots[k] for k in range(2)]
-    member = jnp.where(picks[0] | picks[1], 1.0, 0.0)
-    below = jnp.where(
-        lax.broadcasted_iota(jnp.int32, (tok, tok), 1) < lax.broadcasted_iota(jnp.int32, (tok, tok), 0), 1.0, 0.0
-    ).astype(jnp.bfloat16)
-    rank = jnp.dot(below, member.astype(jnp.bfloat16), preferred_element_type=jnp.float32)
-    place = (member * (rank + 1.0)).astype(jnp.bfloat16)
-    grid = (n_exp, cap, 128)
-    rows = n_exp * cap
-    spread_out = jnp.where(
-        lax.broadcasted_iota(jnp.int32, grid, 0) == lax.broadcasted_iota(jnp.int32, grid, 2), 1.0, 0.0
-    ).reshape(rows, 128)
-    wanted = (lax.broadcasted_iota(jnp.int32, (n_exp, cap, tok), 1) + 1).astype(jnp.float32).reshape(rows, tok)
-    held = lax.dot_general(
-        spread_out.astype(jnp.bfloat16), place, (((1,), (1,)), ((), ())), preferred_element_type=jnp.float32
-    )
-    dispatch = jnp.where(held == wanted, 1.0, 0.0).astype(jnp.bfloat16)
-    sent = jnp.dot(dispatch, normed, preferred_element_type=jnp.float32).astype(jnp.bfloat16)
-    outgoing[...] = sent.reshape(n_exp, cap, width)
-    for i in reversed(range(1, n_exp)):
-        copy = remote(
-            outgoing.at[i], arrived.at[i], out_send.at[i], out_recv.at[i], {"exp": exp_at(offsets[i])}
-        )
-        copy.start()
-        pending.append(copy)
+    group = n_exp // 2
+    for first in (group, 0):
+        sent = jnp.dot(
+            dispatch[first * cap : (first + group) * cap], normed, preferred_element_type=jnp.float32
+        ).astype(jnp.bfloat16)
+        outgoing[first : first + group] = sent.reshape(group, cap, width)
+        for i in reversed(range(max(first, 1), first + group)):
+            copy = remote(
+                outgoing.at[i], arrived.at[i], out_send.at[i], out_recv.at[i], {"exp": exp_at(offsets[i])}
+            )
+            copy.start()
+            pending.append(copy)
     arrived[0] = outgoing[0]
 
     affinity = jax.nn.sigmoid(
@@ -259,13 +276,16 @@
         jnp.sum(jnp.where(expert_lane == ids[:, k : k + 1], affinity, 0.0), axis=1, keepdims=True) for k in range(2)
     ]
     both = picked[0] + picked[1]
-    column = lax.broadcasted_iota(jnp.int32, (tok, rows), 1).astype(jnp.float32)
     combine = jnp.zeros((tok, rows), jnp.float32)
     for k in range(2):
-        own_rank = jnp.sum(jnp.where(picks[k], rank, 0.0), axis=1, keepdims=True)
-        target = slots[k].astype(jnp.float32) * cap + own_rank
-        combine = combine + jnp.where(column == target, picked[k] / both, 0.0)
-    combine = combine.astype(jnp.bfloat16)
+        combine = combine + chosen[k] * (picked[k] / both)
+    combine_part[...] = combine.astype(jnp.bfloat16)
+    results = [
+        pltpu.make_async_copy(hidden_part, hidden_out, local_sem.at[9]),
+        pltpu.make_async_copy(combine_part, combine_out, local_sem.at[10]),
+    ]
+    for copy in results:
+        copy.start()
 
     for copy in first_half:
         copy.wait_send()
@@ -275,9 +295,10 @@
     from_sibling(*gate_views[0])
     from_sibling(*gate_views[1])
     ff = activation.shape[1]
-    group = n_exp // 2
     chunk = 256
-    for first in range(0, n_exp, group):
+    for first in (0, group):
+        if first == group:
+            forward(dbuf, d_send, d_recv)
         for i in range(max(first, 1), first + group):
             remote(
                 outgoing.at[i], arrived.at[i], out_send.at[i], out_recv.at[i], {"exp": exp_at(offsets[i])}
@@ -293,7 +314,6 @@
             activation[first * cap : (first + group) * cap, f : f + chunk] = (
                 gate / (1.0 + jnp.exp(-gate)) * up
             ).astype(jnp.bfloat16)
-    forward(dbuf, d_send, d_recv)
     from_sibling(dbuf, d_send, d_recv)
     for first in (group, 0):
         made = jnp.dot(
@@ -312,11 +332,13 @@
             )
             copy.start()
             pending.append(copy)
-    returned[0] = produced[0]
+    own = pltpu.make_async_copy(produced.at[0], returned.at[0], local_sem.at[11])
+    own.start()
+    results.append(own)
     for i in range(1, n_exp):
         remote(produced.at[i], returned.at[i], back_send.at[i], back_recv.at[i], {"exp": exp_at(offsets[i])}).wait_recv()
-    moe = jnp.dot(combine, returned[...].reshape(rows, width), preferred_element_type=jnp.float32)
-    out[0] = (wide + moe).astype(jnp.bfloat16)
+    for copy in results:
+        copy.wait()
     for copy in pending:
         copy.wait_send()
 
@@ -333,17 +355,20 @@
     depth, twice_ff = expert_gate_up.shape[1:]
     ff_part = expert_down.shape[1]
     half = out_proj.shape[0] // 2
-    vmem = pl.BlockSpec(memory_space=pltpu.VMEM)
     anywhere = pl.BlockSpec(memory_space=pl.ANY)
     dma = pltpu.SemaphoreType.DMA
     ctx_sems = [dma((2 * chips,)), dma((n_ctx,))]
     rows = n_exp * cap
     groups = 4
-    return pl.pallas_call(
+    returned, hidden, combine = pl.pallas_call(
         functools.partial(fused, n_ctx, n_exp, cap),
-        out_shape=jax.ShapeDtypeStruct(residual.shape, bf16),
+        out_shape=[
+            jax.ShapeDtypeStruct((n_exp, cap, width), bf16),
+            jax.ShapeDtypeStruct((tok, width), bf16),
+            jax.ShapeDtypeStruct((tok, rows), bf16),
+        ],
         in_specs=[anywhere] * 9,
-        out_specs=vmem,
+        out_specs=[anywhere] * 3,
         scratch_shapes=[
             pltpu.VMEM((tok, width), bf16),
             pltpu.VMEM((tok, width), bf16),
@@ -356,10 +381,13 @@
             pltpu.VMEM((n_exp, cap, width), bf16),
             pltpu.VMEM((n_exp, cap, width), bf16),
             pltpu.VMEM((n_exp, cap, width), bf16),
-            pltpu.VMEM((n_exp, cap, width), bf16),
+            pltpu.VMEM((rows, tok), bf16),
+            pltpu.VMEM((2, tok, rows), jnp.float32),
+            pltpu.VMEM((tok, width), bf16),
+            pltpu.VMEM((tok, rows), bf16),
             pltpu.VMEM((tok, width), bf16),
             pltpu.VMEM((rows, twice_ff // 2), bf16),
-            dma((9,)),
+            dma((12,)),
             dma((2 * groups,)),
             dma((2 * groups, 2 * chips)),
             dma((2 * groups, n_ctx)),
@@ -382,6 +410,8 @@
         expert_gate_up,
         expert_down,
     )
+    moe = jnp.dot(combine, returned.reshape(rows, width), preferred_element_type=jnp.float32)
+    return (hidden.astype(jnp.float32) + moe).astype(bf16)[None]
 
 
 def solution(mesh):

time: 71.5 us -> 69.7 us (0.975)
  matrix products: 0 us -> 2.23 us
  Pallas kernels: 68.8 us -> 66.7 us
  local copies, waits for them, and re-layouts: 1.67 us -> 0 us
    dot_general x0 -> x1, matrix products: none -> 2.23 us  [on_device(): jnp.dot(combine, returned.reshape(rows, width), preferred_element_type=jn...]
    pallas_call x1, Pallas kernels: 68.8 us -> 66.7 us  [on_device(): pl.pallas_call(functools.partial(fused, n_ctx, n_exp, cap), out_shape=[ja...]
    unnamed x1 -> x0, local copies, waits for them, and re-layouts: 1.67 us -> none
where the time goes in v4:
time: 69.7 us; the launch traced here: 68.9 us
  Pallas kernels  66.7 us (96%)
  matrix products  2.23 us (3%)
    pallas_call x1, Pallas kernels, on_device(): pl.pallas_call(functools.partial(fused, n_ctx, n_exp, cap), out_shape=[ja...  66.7 us
    dot_general x1, matrix products, on_device(): jnp.dot(combine, returned.reshape(rows, width), preferred_element_type=jn...  2.23 us

profile of v4, /device:TPU:0, one launch (start us, length us, event | category | flops | bytes accessed | tf_op | source)
XLA Modules:
  0.0 68.9 jit_solution(12550048009308228336)
XLA Ops:
  0.0 66.7 %shard_map.91 = (bf16[8,48,1024]{2,1,0:T(8,128)(2,1)}, bf16[128,1024]{1,0:T(8,128)(2,1)}, bf16[128,384]{1,0:T(8,128)(2,1)}) custom-call(bf16[1,128,1024]{2,1,0:T(8,128)(2,1)} %residual_in.1, bf16[1,128,1024]{2,1,0:T(8,128)(2,1)} %query_in.1, bf16[8,1024]{1,0:T(8,128)(2,1)} %bitcast.8, s32[1,2,128]{2,1,0:T(2,128)} %bitcast.9, bf16[1,128,1024]{2,1,0:T(8,128)(2,1)} %key.1, ...), custom_call_target="tpu_custom_call" | custom-call | tf_op jit(solution)/shard_map/pallas_call | solution.py:363
  66.7 2.2 %fusion.1 = bf16[1,128,1024]{2,1,0:T(8,128)(2,1)} fusion(bf16[128,384]{1,0:T(8,128)(2,1)} %get-tuple-element.9, bf16[384,1024]{1,0:T(8,128)(2,1)} %bitcast.7, bf16[128,1024]{1,0:T(8,128)(2,1)} %get-tuple-element.8), kind=kOutput, calls=%fused_computation.2 | convolution fusion | flops 101056512 | bytes 1409024 | tf_op jit(solution)/shard_map/dot_general | solution.py:413

commit v5 on v4

--- a/solution.py
+++ b/solution.py
@@ -47,9 +47,21 @@
     context,
     activation,
     local_sem,
+    queries_in,
+    part_out,
+    part_in,
+    stat_out,
+    stat_in,
+    own_part,
     kv_local,
     kv_send,
     kv_recv,
+    q_send,
+    q_recv,
+    part_send,
+    part_recv,
+    stat_send,
+    stat_recv,
     g_send,
     g_recv,
     d_send,
@@ -69,8 +81,6 @@
     core = lax.rem(c, 2)
     sibling = chip * 2 + 1 - core
     tok, width = query.shape
-    groups = kvbuf.shape[1] // 2
-    group_cols = kvbuf.shape[3]
     half = out_proj.shape[0] // 2
     part_depth = gbuf.shape[2]
 
@@ -98,12 +108,8 @@
         pltpu.make_async_copy(router_in, router, local_sem.at[6]),
         pltpu.make_async_copy(ids_in.at[0], ids_ref, local_sem.at[7]),
     ]
-    kv_parts = []
-    for g in range(groups):
-        for ref in (key, value):
-            kv_parts.append(ref.at[0, :, pl.ds(g * group_cols, group_cols)])
-    for i, part in enumerate(kv_parts):
-        locals_.append(pltpu.make_async_copy(part, kvbuf.at[c, i], kv_local.at[i]))
+    for i, ref in enumerate((key, value)):
+        locals_.append(pltpu.make_async_copy(ref.at[0], kvbuf.at[i, core], kv_local.at[i]))
     for copy in locals_:
         copy.start()
     pl.semaphore_wait(barrier, n_exp - 1 + chips - 1 + 1)
@@ -139,14 +145,29 @@
         for r in range(chips):
             landed(buf, send, recv, lax.rem(chip + r, chips) * 2 + 1 - core)
 
-    kv_copies = {}
-    kv_views = [(kvbuf.at[:, i], kv_send.at[i], kv_recv.at[i]) for i in range(2 * groups)]
-
-    def send_group(g):
-        kv_copies[g] = spread(kv_parts[2 * g], *kv_views[2 * g]) + spread(kv_parts[2 * g + 1], *kv_views[2 * g + 1])
-
-    send_group(0)
-    send_group(1)
+    for i, ref in enumerate((key, value)):
+        copy = remote(ref.at[0], kvbuf.at[i, core], kv_send.at[i], kv_recv.at[i], {"ctx": sibling})
+        copy.start()
+        pending.append(copy)
+
+    def ask(r):
+        return remote(
+            query_in.at[0], queries_in.at[r], q_send.at[r], q_recv.at[r], {"ctx": chip_at(chips - r)}
+        )
+
+    def answer(r):
+        where = {"ctx": chip_at(r)}
+        return (
+            remote(part_out.at[r], part_in.at[r], part_send.at[r], part_recv.at[r], where),
+            remote(stat_out.at[r], stat_in.at[r], stat_send.at[r], stat_recv.at[r], where),
+        )
+
+    for r in range(1, chips):
+
+        @pl.when(chip >= r)
+        def _(r=r):
+            ask(r).start()
+
     offsets = [0]
     for r in range(1, n_exp // 2 + 1):
         offsets.append(r)
@@ -206,42 +227,99 @@
         target = slots[k].astype(jnp.float32) * cap + own_rank
         chosen[k] = jnp.where(column == target, 1.0, 0.0)
 
-    keys = n_ctx * tok
-    q_pos = c * tok + lax.broadcasted_iota(jnp.int32, (tok, keys), 0)
-    k_pos = lax.broadcasted_iota(jnp.int32, (tok, keys), 1)
-    allowed = k_pos <= q_pos
-    for g in range(groups):
-        forward(*kv_views[2 * g])
-        forward(*kv_views[2 * g + 1])
-        for copy in kv_copies[g]:
-            copy.wait_send()
-        if g + 2 < groups:
-            send_group(g + 2)
-        if g == groups - 2:
-            first_half = spread(gate_parts[0], *gate_views[0])
-        if g == groups - 1:
-            pending.extend(spread(gate_parts[1], *gate_views[1]))
-            for r in offsets[1:]:
-                s = exp_at(r)
-                proj_at(s, core).wait_recv()
-                copy = proj_at(s, core)
+    for r in range(1, chips):
+
+        @pl.when(chip >= r)
+        def _(r=r):
+            ask(r).wait_send()
+
+    first_half = spread(gate_parts[0], *gate_views[0])
+    for i in range(2):
+        remote(kvbuf.at[i, 0], kvbuf.at[i, 0], kv_send.at[i], kv_recv.at[i], {"ctx": sibling}).wait_recv()
+
+    keys = 2 * tok
+    stat_lane = lax.broadcasted_iota(jnp.int32, (tok, 128), 1)
+    allowed = lax.broadcasted_iota(jnp.int32, (tok, keys), 1) <= core * tok + lax.broadcasted_iota(
+        jnp.int32, (tok, keys), 0
+    )
+
+    def attend(asked, mask, keep):
+        stats = jnp.zeros((tok, 128), jnp.float32)
+        for h in range(HEADS):
+            cols = slice(h * HEAD_DIM, (h + 1) * HEAD_DIM)
+            scores = lax.dot_general(
+                asked(cols),
+                kvbuf[0, :, :, cols].reshape(keys, HEAD_DIM),
+                (((1,), (1,)), ((), ())),
+                preferred_element_type=jnp.float32,
+            ) * (HEAD_DIM**-0.5)
+            if mask:
+                scores = jnp.where(allowed, scores, NEG_FILL)
+            top = jnp.max(scores, axis=1, keepdims=True)
+            weights = jnp.exp(scores - top)
+            total = jnp.sum(weights, axis=1, keepdims=True)
+            part = jnp.dot(
+                weights.astype(jnp.bfloat16),
+                kvbuf[1, :, :, cols].reshape(keys, HEAD_DIM),
+                preferred_element_type=jnp.float32,
+            )
+            keep(cols, part / total)
+            stats = jnp.where(stat_lane == h, top, jnp.where(stat_lane == 64 + h, total, stats))
+        return stats
+
+    for r in range(1, chips):
+
+        @pl.when(chip + r < chips)
+        def _(r=r):
+            ask(r).wait_recv()
+
+            def keep(cols, part):
+                part_out[r, :, cols] = part.astype(jnp.bfloat16)
+
+            stat_out[r] = attend(lambda cols: queries_in[r, :, cols], False, keep)
+            for copy in answer(r):
                 copy.start()
-                pending.append(copy)
-        from_sibling(*kv_views[2 * g])
-        from_sibling(*kv_views[2 * g + 1])
-        for h in range(group_cols // HEAD_DIM):
-            inner = slice(h * HEAD_DIM, (h + 1) * HEAD_DIM)
-            cols = slice(g * group_cols + h * HEAD_DIM, g * group_cols + (h + 1) * HEAD_DIM)
-            k_head = kvbuf[:, 2 * g, :, inner].reshape(keys, HEAD_DIM)
-            v_head = kvbuf[:, 2 * g + 1, :, inner].reshape(keys, HEAD_DIM)
-            scores = lax.dot_general(
-                query[:, cols], k_head, (((1,), (1,)), ((), ())), preferred_element_type=jnp.float32
-            )
-            scores = jnp.where(allowed, scores * (HEAD_DIM**-0.5), NEG_FILL)
-            weights = jnp.exp(scores - jnp.max(scores, axis=1, keepdims=True))
-            total = jnp.sum(weights, axis=1, keepdims=True)
-            part = jnp.dot(weights.astype(jnp.bfloat16), v_head, preferred_element_type=jnp.float32)
-            context[:, cols] = (part / total).astype(jnp.bfloat16)
+
+        @pl.when(chip < r)
+        def _(r=r):
+            part_in[r] = jnp.zeros((tok, width), jnp.bfloat16)
+            stat_in[r] = jnp.where(stat_lane < 64, NEG_FILL, 0.0)
+
+    def keep_own(cols, part):
+        own_part[:, cols] = part
+
+    stat_out[0] = attend(lambda cols: query[:, cols], True, keep_own)
+    for r in range(1, chips):
+
+        @pl.when(chip + r < chips)
+        def _(r=r):
+            for copy in answer(r):
+                copy.wait_send()
+
+    pending.extend(spread(gate_parts[1], *gate_views[1]))
+    for r in offsets[1:]:
+        s = exp_at(r)
+        proj_at(s, core).wait_recv()
+        copy = proj_at(s, core)
+        copy.start()
+        pending.append(copy)
+    for r in range(1, chips):
+
+        @pl.when(chip >= r)
+        def _(r=r):
+            for copy in answer(r):
+                copy.wait_recv()
+
+    all_stats = [stat_out[0]] + [stat_in[r] for r in range(1, chips)]
+    for h in range(HEADS):
+        cols = slice(h * HEAD_DIM, (h + 1) * HEAD_DIM)
+        tops = [stat[:, h : h + 1] for stat in all_stats]
+        highest = functools.reduce(jnp.maximum, tops)
+        shares = [jnp.exp(top - highest) * stat[:, 64 + h : 65 + h] for top, stat in zip(tops, all_stats)]
+        summed = shares[0] * own_part[:, cols]
+        for r in range(1, chips):
+            summed = summed + shares[r] * part_in[r, :, cols].astype(jnp.float32)
+        context[:, cols] = (summed / functools.reduce(jnp.add, shares)).astype(jnp.bfloat16)
 
     for r in offsets[1:]:
         proj_at(exp_at(r), 1 - core).wait_recv()
@@ -359,7 +437,6 @@
     dma = pltpu.SemaphoreType.DMA
     ctx_sems = [dma((2 * chips,)), dma((n_ctx,))]
     rows = n_exp * cap
-    groups = 4
     returned, hidden, combine = pl.pallas_call(
         functools.partial(fused, n_ctx, n_exp, cap),
         out_shape=[
@@ -374,7 +451,7 @@
             pltpu.VMEM((tok, width), bf16),
             pltpu.VMEM((n_exp, width), bf16),
             pltpu.VMEM((2, tok), jnp.int32),
-            pltpu.VMEM((n_ctx, 2 * groups, tok, width // groups), bf16),
+            pltpu.VMEM((2, 2, tok, width), bf16),
             pltpu.VMEM((n_exp, 2, half, width), bf16),
             pltpu.VMEM((n_ctx, 2, depth // 2, twice_ff), bf16),
             pltpu.VMEM((n_ctx, ff_part, width), bf16),
@@ -388,10 +465,17 @@
             pltpu.VMEM((tok, width), bf16),
             pltpu.VMEM((rows, twice_ff // 2), bf16),
             dma((12,)),
-            dma((2 * groups,)),
-            dma((2 * groups, 2 * chips)),
-            dma((2 * groups, n_ctx)),
+            pltpu.VMEM((chips, tok, width), bf16),
+            pltpu.VMEM((chips, tok, width), bf16),
+            pltpu.VMEM((chips, tok, width), bf16),
+            pltpu.VMEM((chips, tok, 128), jnp.float32),
+            pltpu.VMEM((chips, tok, 128), jnp.float32),
+            pltpu.VMEM((tok, width), jnp.float32),
+            dma((2,)),
+            dma((2,)),
+            dma((2,)),
         ]
+        + [dma((chips,))] * 6
         + [dma((2, 2 * chips)), dma((2, n_ctx))]
         + ctx_sems
         + [dma((n_exp,)), dma((n_exp, 2)), dma((n_exp,))]

time: 69.7 us -> 69.3 us (level)
  no operation moved by 1% of the time
where the time goes in v5:
time: 69.3 us; the launch traced here: 68.3 us
  Pallas kernels  66.1 us (95%)
  matrix products  2.23 us (3%)
    pallas_call x1, Pallas kernels, on_device(): pl.pallas_call(functools.partial(fused, n_ctx, n_exp, cap), out_shape=[ja...  66.1 us
    dot_general x1, matrix products, on_device(): jnp.dot(combine, returned.reshape(rows, width), preferred_element_type=jn...  2.23 us

profile of v5, /device:TPU:0, one launch (start us, length us, event | category | flops | bytes accessed | tf_op | source)
XLA Modules:
  0.0 68.3 jit_solution(13210511373795524327)
XLA Ops:
  0.0 66.1 %shard_map.91 = (bf16[8,48,1024]{2,1,0:T(8,128)(2,1)}, bf16[128,1024]{1,0:T(8,128)(2,1)}, bf16[128,384]{1,0:T(8,128)(2,1)}) custom-call(bf16[1,128,1024]{2,1,0:T(8,128)(2,1)} %residual_in.1, bf16[1,128,1024]{2,1,0:T(8,128)(2,1)} %query_in.1, bf16[8,1024]{1,0:T(8,128)(2,1)} %bitcast.8, s32[1,2,128]{2,1,0:T(2,128)} %bitcast.9, bf16[1,128,1024]{2,1,0:T(8,128)(2,1)} %key.1, ...), custom_call_target="tpu_custom_call" | custom-call | tf_op jit(solution)/shard_map/pallas_call | solution.py:440
  66.1 2.2 %fusion.1 = bf16[1,128,1024]{2,1,0:T(8,128)(2,1)} fusion(bf16[128,384]{1,0:T(8,128)(2,1)} %get-tuple-element.9, bf16[384,1024]{1,0:T(8,128)(2,1)} %bitcast.7, bf16[128,1024]{1,0:T(8,128)(2,1)} %get-tuple-element.8), kind=kOutput, calls=%fused_computation.2 | convolution fusion | flops 101056512 | bytes 1409024 | tf_op jit(solution)/shard_map/dot_general | solution.py:497

commit v6 on v5

--- a/solution.py
+++ b/solution.py
@@ -393,14 +393,15 @@
                 gate / (1.0 + jnp.exp(-gate)) * up
             ).astype(jnp.bfloat16)
     from_sibling(dbuf, d_send, d_recv)
-    for first in (group, 0):
+    quarter = n_exp // 4
+    for first in reversed(range(0, n_exp, quarter)):
         made = jnp.dot(
-            activation[first * cap : (first + group) * cap],
+            activation[first * cap : (first + quarter) * cap],
             dbuf[...].reshape(ff, width),
             preferred_element_type=jnp.float32,
         )
-        produced[first : first + group] = made.astype(jnp.bfloat16).reshape(group, cap, width)
-        for i in reversed(range(max(first, 1), first + group)):
+        produced[first : first + quarter] = made.astype(jnp.bfloat16).reshape(quarter, cap, width)
+        for i in reversed(range(max(first, 1), first + quarter)):
             copy = remote(
                 produced.at[i],
                 returned.at[i],

time: 69.3 us -> 69.2 us (level)
  no operation moved by 1% of the time
where the time goes in v6:
time: 69.2 us; the launch traced here: 68.2 us
  Pallas kernels  66 us (95%)
  matrix products  2.23 us (3%)
    pallas_call x1, Pallas kernels, on_device(): pl.pallas_call(functools.partial(fused, n_ctx, n_exp, cap), out_shape=[ja...  66 us
    dot_general x1, matrix products, on_device(): jnp.dot(combine, returned.reshape(rows, width), preferred_element_type=jn...  2.23 us

profile of v6, /device:TPU:0, one launch (start us, length us, event | category | flops | bytes accessed | tf_op | source)
XLA Modules:
  0.0 68.2 jit_solution(3939934148195823204)
XLA Ops:
  0.0 66.0 %shard_map.91 = (bf16[8,48,1024]{2,1,0:T(8,128)(2,1)}, bf16[128,1024]{1,0:T(8,128)(2,1)}, bf16[128,384]{1,0:T(8,128)(2,1)}) custom-call(bf16[1,128,1024]{2,1,0:T(8,128)(2,1)} %residual_in.1, bf16[1,128,1024]{2,1,0:T(8,128)(2,1)} %query_in.1, bf16[8,1024]{1,0:T(8,128)(2,1)} %bitcast.8, s32[1,2,128]{2,1,0:T(2,128)} %bitcast.9, bf16[1,128,1024]{2,1,0:T(8,128)(2,1)} %key.1, ...), custom_call_target="tpu_custom_call" | custom-call | tf_op jit(solution)/shard_map/pallas_call | solution.py:441
  66.0 2.2 %fusion.1 = bf16[1,128,1024]{2,1,0:T(8,128)(2,1)} fusion(bf16[128,384]{1,0:T(8,128)(2,1)} %get-tuple-element.9, bf16[384,1024]{1,0:T(8,128)(2,1)} %bitcast.7, bf16[128,1024]{1,0:T(8,128)(2,1)} %get-tuple-element.8), kind=kOutput, calls=%fused_computation.2 | convolution fusion | flops 101056512 | bytes 1409024 | tf_op jit(solution)/shard_map/dot_general | solution.py:498
